TPU v7x, 32 devices: a whole 2x2x4 slice. The times are simulated.
32 devices in a mesh: seq: 2 (over y), dp: 16 (over z, x, core).
Axes of the slice: x: 2, y: 2, z: 4, core: 2. Of those that a mesh axis runs over, the one named last changes fastest.
Arguments:
- tokens: bfloat16 [16, 1024, 768], P('dp', 'seq'), may hold values from -6 to 6
- first_values: bfloat16 [16, 1024, 384], P('dp', 'seq'), may hold values from -6 to 6
- out_grad: bfloat16 [16, 1024, 768], P('dp', 'seq'), may hold values from -6 to 6
- block_place: int32 [16, 4], P('dp'), may hold values from 0 to 3, each once within a row
- owners: int32 [414], replicated, may hold values from 0 to 15, as said below
- masters: float32 [640, 16384], P('dp'), as said below
- moment_one: float32 [640, 16384], P('dp')
- moment_two: float32 [640, 16384], P('dp'), as said below
- vector_master: float32 [8832], replicated
- vector_moment_one: float32 [8832], replicated
- vector_moment_two: float32 [8832], replicated, as said below
Outputs:
- output: bfloat16 [16, 1024, 768], P('dp', 'seq')
- tokens_grad: float32 [16, 1024, 768], P('dp', 'seq')
- first_grad: float32 [16, 1024, 384], P('dp', 'seq')
- new_masters: float32 [640, 16384], P('dp')
- new_moment_one: float32 [640, 16384], P('dp')
- new_moment_two: float32 [640, 16384], P('dp')
- new_copies: bfloat16 [640, 16384], P('dp')
- new_vector: float32 [8832], replicated
- new_vector_one: float32 [8832], replicated
- new_vector_two: float32 [8832], replicated
Inputs may be any that keep to these rules, and one draw needn't show every extreme that they name: `owners`: block t holds entries t * 16384 onward of the six weight matrices laid end to end; no index of dp keeps more than 40 blocks, and one keeps exactly 40. `block_place`: each row orders the 4 blocks of one sequence. `masters`: rows that no block is placed in are unused slots. `moment_two`: Positive. `vector_moment_two`: Positive.
All inputs are finite; a program needn't handle non-finite values.
Results may differ from a plain program's by a relative error of at most 0.011.
Values may be sent and summed in bfloat16 or wider, within the bound.
A program may use at most 256 MiB of HBM per device.

v0:
```python
import jax
import jax.numpy as jnp
from jax import lax
from jax.sharding import PartitionSpec as P

D = 768
HD = 64
FF = 3072
STEP = 10
HV = 384


EPS_NORM = 1e-05
EPS_ADAM = 1e-08
BETA_ONE = 0.5
BETA_TWO = 0.5
RATE_MATRIX = 0.03
RATE_VECTOR = 0.25
DECAY_MATRIX = 0.1


def from_partner(value, axis, distance):
    mask = 2**distance
    pairs = [(source, source ^ mask) for source in range(lax.axis_size(axis))]
    return lax.ppermute(value, axis, pairs)


def layer_norm(values, norm_gain, norm_shift):
    center = jnp.mean(values, axis=-1, keepdims=True)
    centred = values - center
    spread = jnp.mean(centred * centred, axis=-1, keepdims=True)
    return centred * lax.rsqrt(spread + EPS_NORM) * norm_gain + norm_shift


def gelu_tanh(values):
    return (
        0.5
        * values
        * (1.0 + jnp.tanh(0.7978845608028654 * (values + 0.044715 * values * values * values)))
    )


def slot_numbers(owners):
    tile_order = jnp.arange(owners.shape[0], dtype=jnp.int32)
    earlier = (owners[None, :] == owners[:, None]) & (tile_order[None, :] < tile_order[:, None])
    return jnp.sum(earlier.astype(jnp.int32), axis=1)


def split_weights(flat):
    lengths = [D * D, D * D, D * HV, D * D, D * FF, FF * D]
    matrix_shapes = [(D, D), (D, D), (D, HV), (D, D), (D, FF), (FF, D)]
    pieces = []
    offset = 0
    for length, matrix_shape in zip(lengths, matrix_shapes):
        pieces.append(flat[offset : offset + length].reshape(matrix_shape))
        offset = offset + length
    return pieces


def split_vector(vector):
    pieces = [vector[i * D : (i + 1) * D] for i in range(7)]
    pieces.append(vector[7 * D : 7 * D + HV])
    pieces.append(vector[7 * D + HV :])
    return pieces


def adam_step(weight, first_moment, second_moment, gradient, step_rate, weight_decay):
    first_new = BETA_ONE * first_moment + (1.0 - BETA_ONE) * gradient
    second_new = BETA_TWO * second_moment + (1.0 - BETA_TWO) * gradient * gradient
    first_fix = 1.0 - BETA_ONE**STEP
    second_fix = 1.0 - BETA_TWO**STEP
    update = first_new / first_fix / (jnp.sqrt(second_new / second_fix) + EPS_ADAM)
    return (weight - step_rate * (update + weight_decay * weight), first_new, second_new)


def inverse_of(slot_rows, slot_total):
    tile_count = slot_rows.shape[0]
    return (
        jnp.full((slot_total,), tile_count, jnp.int32)
        .at[slot_rows]
        .set(jnp.arange(tile_count, dtype=jnp.int32))
    )


def masked_scores(query_part, key_part, near_pos, all_pos):
    scores = jnp.einsum(
        "qhd,khd->hqk", query_part, key_part, preferred_element_type=jnp.float32
    ) * HD ** (-0.5)
    allowed = all_pos[None, :] <= near_pos[:, None]
    return jnp.where(allowed[None], scores, -1e30)


def attend_block(packed):
    query_seq, key_seq, value_seq, near_pos, all_pos = packed
    value_heads = HV // HD
    outputs = []
    log_parts = []
    for head_group in range(2):
        columns = slice(head_group * HV, (head_group + 1) * HV)
        query_part = query_seq[:, columns].reshape(-1, value_heads, HD)
        key_part = key_seq[:, columns].reshape(-1, value_heads, HD)
        value_part = value_seq[:, columns].reshape(-1, value_heads, HD)
        scores = masked_scores(query_part, key_part, near_pos, all_pos)
        row_top = jnp.max(scores, axis=-1, keepdims=True)
        exponent = jnp.exp(scores - row_top)
        row_sum = jnp.sum(exponent, axis=-1, keepdims=True)
        weights_low = (exponent / row_sum).astype(jnp.bfloat16)
        mixed = jnp.einsum(
            "hqk,khd->qhd", weights_low, value_part, preferred_element_type=jnp.float32
        )
        outputs.append(mixed.reshape(-1, HV))
        log_parts.append((row_top + jnp.log(row_sum))[..., 0])
    return (jnp.concatenate(outputs, axis=1), jnp.concatenate(log_parts, axis=0))


def attend_back(packed):
    query_seq, key_seq, value_seq, near_pos, all_pos, log_total, grad_seq = packed
    value_heads = HV // HD
    query_grads = []
    key_grads = []
    value_grads = []
    for head_group in range(2):
        columns = slice(head_group * HV, (head_group + 1) * HV)
        query_part = query_seq[:, columns].reshape(-1, value_heads, HD)
        key_part = key_seq[:, columns].reshape(-1, value_heads, HD)
        value_part = value_seq[:, columns].reshape(-1, value_heads, HD)
        grad_part = grad_seq[:, columns].reshape(-1, value_heads, HD)
        scores = masked_scores(query_part, key_part, near_pos, all_pos)
        log_part = log_total[head_group * value_heads : (head_group + 1) * value_heads]
        chance = jnp.exp(scores - log_part[..., None])
        grad_chance = jnp.einsum(
            "qhd,khd->hqk", grad_part, value_part, preferred_element_type=jnp.float32
        )
        grad_value = jnp.einsum(
            "hqk,qhd->khd",
            chance.astype(jnp.bfloat16),
            grad_part,
            preferred_element_type=jnp.float32,
        )
        grad_score = (
            chance * (grad_chance - jnp.sum(chance * grad_chance, axis=-1, keepdims=True))
        ).astype(jnp.bfloat16)
        grad_query = jnp.einsum(
            "hqk,khd->qhd", grad_score, key_part, preferred_element_type=jnp.float32
        ) * HD ** (-0.5)
        grad_key = jnp.einsum(
            "hqk,qhd->khd", grad_score, query_part, preferred_element_type=jnp.float32
        ) * HD ** (-0.5)
        query_grads.append(grad_query.reshape(-1, HV))
        key_grads.append(grad_key.reshape(-1, HV))
        value_grads.append(grad_value.reshape(-1, HV))
    return (
        jnp.concatenate(query_grads, axis=1),
        jnp.concatenate(key_grads, axis=1),
        jnp.concatenate(value_grads, axis=1),
    )


def shards(
    tokens,
    first_values,
    out_grad,
    block_place,
    owners,
    masters,
    moment_one,
    moment_two,
    vector_master,
    vector_moment_one,
    vector_moment_two,
):
    capacity = masters.shape[0]
    tile_len = masters.shape[1]
    dp_count = lax.axis_size("dp")
    tile_count = owners.shape[0]
    slot_index = slot_numbers(owners)
    owner_inverse = inverse_of(owners * capacity + slot_index, capacity * dp_count)
    tiles = (
        jnp.zeros((tile_count, tile_len), jnp.bfloat16)
        .at[owner_inverse]
        .set(lax.all_gather(masters.astype(jnp.bfloat16), "dp", axis=0, tiled=True), mode="drop")
    )
    w_query, w_key, w_value, w_out, w_up, w_down = split_weights(tiles.reshape(-1))
    (
        gain_one,
        shift_one,
        gain_two,
        shift_two,
        bias_query,
        bias_out,
        bias_down,
        bias_value,
        bias_up,
    ) = split_vector(vector_master)
    seq_count = lax.axis_size("seq")
    seq_here = lax.axis_index("seq")
    seqs_here, half_len, model_width = tokens.shape
    row_count = seqs_here * half_len
    per_device = block_place.shape[1] // seq_count
    block_len = half_len // per_device
    near_blocks = lax.dynamic_slice_in_dim(block_place, seq_here * per_device, per_device, 1)
    far_blocks = lax.dynamic_slice_in_dim(block_place, (1 - seq_here) * per_device, per_device, 1)
    within = jnp.arange(half_len, dtype=jnp.int32) % block_len
    near_pos = jnp.repeat(near_blocks, block_len, axis=1) * block_len + within[None, :]
    far_pos = jnp.repeat(far_blocks, block_len, axis=1) * block_len + within[None, :]
    all_pos = jnp.concatenate([near_pos, far_pos], axis=1)
    inputs = tokens.reshape(row_count, model_width).astype(jnp.float32)
    normed_one, norm_one_back = jax.vjp(layer_norm, inputs, gain_one, shift_one)
    normed_low = normed_one.astype(jnp.bfloat16)
    query_rows = (
        jnp.dot(normed_low, w_query, preferred_element_type=jnp.float32) + bias_query
    ).astype(jnp.bfloat16)
    key_rows = jnp.dot(normed_low, w_key, preferred_element_type=jnp.float32).astype(jnp.bfloat16)
    fresh_rows = (
        jnp.dot(normed_low, w_value, preferred_element_type=jnp.float32) + bias_value
    ).astype(jnp.bfloat16)
    value_rows = jnp.concatenate([fresh_rows, first_values.reshape(row_count, HV)], axis=1)
    key_far, value_far = from_partner((key_rows, value_rows), "seq", 0)
    seq_view = (seqs_here, half_len, model_width)
    key_all = jnp.concatenate([key_rows.reshape(seq_view), key_far.reshape(seq_view)], axis=1)
    value_all = jnp.concatenate([value_rows.reshape(seq_view), value_far.reshape(seq_view)], axis=1)
    query_view = query_rows.reshape(seq_view)
    attended, log_total = lax.map(attend_block, (query_view, key_all, value_all, near_pos, all_pos))
    attended_low = attended.reshape(row_count, model_width).astype(jnp.bfloat16)
    resid = inputs + jnp.dot(attended_low, w_out, preferred_element_type=jnp.float32) + bias_out
    normed_two, norm_two_back = jax.vjp(layer_norm, resid, gain_two, shift_two)
    normed_two_low = normed_two.astype(jnp.bfloat16)
    hidden_pre = jnp.dot(normed_two_low, w_up, preferred_element_type=jnp.float32) + bias_up
    hidden_act, gelu_back = jax.vjp(gelu_tanh, hidden_pre)
    hidden_low = hidden_act.astype(jnp.bfloat16)
    result = resid + jnp.dot(hidden_low, w_down, preferred_element_type=jnp.float32) + bias_down
    grad_result = out_grad.reshape(row_count, model_width)
    grad_w_down = jnp.einsum(
        "rf,rd->fd", hidden_low, grad_result, preferred_element_type=jnp.float32
    )
    grad_bias_down = jnp.sum(grad_result.astype(jnp.float32), axis=0)
    grad_act = jnp.einsum("rd,fd->rf", grad_result, w_down, preferred_element_type=jnp.float32)
    grad_pre_low = gelu_back(grad_act)[0].astype(jnp.bfloat16)
    grad_bias_up = jnp.sum(grad_pre_low.astype(jnp.float32), axis=0)
    grad_w_up = jnp.einsum(
        "rd,rf->df", normed_two_low, grad_pre_low, preferred_element_type=jnp.float32
    )
    grad_normed_two = jnp.einsum(
        "rf,df->rd", grad_pre_low, w_up, preferred_element_type=jnp.float32
    )
    grad_resid_norm, grad_gain_two, grad_shift_two = norm_two_back(grad_normed_two)
    grad_resid = grad_result.astype(jnp.float32) + grad_resid_norm
    grad_resid_low = grad_resid.astype(jnp.bfloat16)
    grad_bias_out = jnp.sum(grad_resid_low.astype(jnp.float32), axis=0)
    grad_w_out = jnp.einsum(
        "re,rd->ed", attended_low, grad_resid_low, preferred_element_type=jnp.float32
    )
    grad_attended = jnp.einsum(
        "rd,ed->re", grad_resid_low, w_out, preferred_element_type=jnp.float32
    ).astype(jnp.bfloat16)
    grad_query, grad_key_all, grad_value_all = lax.map(
        attend_back,
        (
            query_view,
            key_all,
            value_all,
            near_pos,
            all_pos,
            log_total,
            grad_attended.reshape(seq_view),
        ),
    )
    key_back, value_back = from_partner(
        (
            grad_key_all[:, half_len:].reshape(row_count, model_width),
            grad_value_all[:, half_len:].reshape(row_count, model_width),
        ),
        "seq",
        0,
    )
    grad_key = grad_key_all[:, :half_len].reshape(row_count, model_width) + key_back
    grad_value = grad_value_all[:, :half_len].reshape(row_count, model_width) + value_back
    grad_query_low = grad_query.reshape(row_count, model_width).astype(jnp.bfloat16)
    grad_key_low = grad_key.astype(jnp.bfloat16)
    grad_fresh_low = grad_value[:, :HV].astype(jnp.bfloat16)
    first_grad = grad_value[:, HV:]
    grad_bias_query = jnp.sum(grad_query_low.astype(jnp.float32), axis=0)
    grad_bias_value = jnp.sum(grad_fresh_low.astype(jnp.float32), axis=0)
    grad_w_query = jnp.einsum(
        "rd,re->de", normed_low, grad_query_low, preferred_element_type=jnp.float32
    )
    grad_w_key = jnp.einsum(
        "rd,re->de", normed_low, grad_key_low, preferred_element_type=jnp.float32
    )
    grad_w_value = jnp.einsum(
        "rd,re->de", normed_low, grad_fresh_low, preferred_element_type=jnp.float32
    )
    grad_normed_one = jnp.einsum(
        "re,de->rd", grad_query_low, w_query, preferred_element_type=jnp.float32
    )
    grad_normed_one = grad_normed_one + jnp.einsum(
        "re,de->rd", grad_key_low, w_key, preferred_element_type=jnp.float32
    )
    grad_normed_one = grad_normed_one + jnp.einsum(
        "re,de->rd", grad_fresh_low, w_value, preferred_element_type=jnp.float32
    )
    grad_input_norm, grad_gain_one, grad_shift_one = norm_one_back(grad_normed_one)
    tokens_grad = grad_resid + grad_input_norm
    grad_tiles = jnp.concatenate(
        [
            grad_w_query.reshape(-1),
            grad_w_key.reshape(-1),
            grad_w_value.reshape(-1),
            grad_w_out.reshape(-1),
            grad_w_up.reshape(-1),
            grad_w_down.reshape(-1),
        ]
    ).reshape(tile_count, tile_len)
    vector_grad = jnp.concatenate(
        [
            grad_gain_one,
            grad_shift_one,
            grad_gain_two,
            grad_shift_two,
            grad_bias_query,
            grad_bias_out,
            grad_bias_down,
            grad_bias_value,
            grad_bias_up,
        ]
    )
    vector_total = lax.psum(vector_grad, ("seq", "dp"))
    picked = jnp.take(grad_tiles, jnp.minimum(owner_inverse, tile_count - 1), axis=0)
    slot_term = jnp.where((owner_inverse < tile_count)[:, None], picked, 0.0)
    received = lax.all_to_all(
        slot_term.reshape(dp_count, capacity, tile_len),
        "dp",
        split_axis=0,
        concat_axis=0,
        tiled=True,
    )
    owned_sum = jnp.sum(received, axis=0)
    reduced = lax.psum(owned_sum, "seq")
    new_master, new_one, new_two = adam_step(
        masters, moment_one, moment_two, reduced, RATE_MATRIX, DECAY_MATRIX
    )
    vector_new, vector_one, vector_two = adam_step(
        vector_master, vector_moment_one, vector_moment_two, vector_total, RATE_VECTOR, 0.0
    )
    return (
        result.astype(jnp.bfloat16).reshape(seq_view),
        tokens_grad.reshape(seq_view),
        first_grad.reshape(seqs_here, half_len, HV),
        new_master,
        new_one,
        new_two,
        new_master.astype(jnp.bfloat16),
        vector_new,
        vector_one,
        vector_two,
    )


def solution(mesh):
    placed = (
        P("dp", "seq", None),
        P("dp", "seq", None),
        P("dp", "seq", None),
        P("dp", None),
        P(),
        P("dp", None),
        P("dp", None),
        P("dp", None),
        P(),
        P(),
        P(),
    )
    return jax.shard_map(
        shards,
        mesh=mesh,
        in_specs=placed,
        out_specs=(
            P("dp", "seq", None),
            P("dp", "seq", None),
            P("dp", "seq", None),
            P("dp", None),
            P("dp", None),
            P("dp", None),
            P("dp", None),
            P(),
            P(),
            P(),
        ),
        check_vma=False,
    )
```

profile of v0, /device:TPU:0, one launch (start us, length us, event | category | flops | bytes accessed | tf_op | source)
XLA Modules:
  0.0 2038.3 jit_solution(2429695387631420291)
XLA Ops:
  19.6 102.5 %all-gather.2.cloned.1.call-done = bf16[640,16384]{1,0:T(8,128)(2,1)} async-done(((bf16[40,16384]{1,0:T(8,128)(2,1)}), bf16[640,16384]{1,0:T(8,128)(2,1)}) %all-gather.2.cloned.1.call-update) | async-done | bytes 20971536 | tf_op jit(solution)/shard_map/all_gather | solution.py:181
  122.0 6.4 broadcast_in_dim.157
  128.5 516.5 %scatter_fusion = bf16[414,16384]{1,0:T(8,128)(2,1)} fusion(bf16[414,16384]{1,0:T(8,128)(2,1)} %broadcast_in_dim.157, s32[640]{0:T(1024)S(1)} %get-tuple-element.114, bf16[640,16384]{1,0:T(8,128)(2,1)} %all-gather.2.cloned.1.call-done), kind=kCustom, calls=%fused_computation.2 | custom fusion | bytes 62917120 | tf_op jit(solution)/shard_map/scatter | solution.py:181
  647.0 4.0 fusion.91
  651.0 9.9 fusion.90
  668.3 3.7 reshape.555
  680.7 9.4 reshape.565
  693.9 9.8 reshape.566
  737.0 8.2 convert_reduce_fusion
  753.5 7.1 fusion.12
  760.6 9.0 multiply_reduce_fusion.1
  769.7 6.2 multiply_convert_fusion.1
  781.4 7.1 fusion.10
  788.5 9.4 multiply_reduce_fusion
  797.8 6.2 multiply_convert_fusion
  831.8 10.4 fusion.52
  846.8 10.9 reshape.588
  857.7 5.3 convolution_bitcast_fusion
  863.0 5.9 copy.57
  875.9 12.1 collective-permute-done.2
  902.8 9.6 constant_dynamic-update-slice_fusion.1
  912.4 3.9 constant_dynamic-update-slice_fusion
  916.3 29.3 %reshape.589 = f32[414,16384]{1,0:T(8,128)} reshape(f32[6782976]{0:T(1024)} %constant_dynamic-update-slice_fusion) | data formatting | bytes 54263808 | tf_op jit(solution)/shard_map/reshape | solution.py:313
  945.6 48.5 %gather_fusion = f32[640,16384]{1,0:T(8,128)} fusion(f32[414,16384]{1,0:T(8,128)} %reshape.589, s32[1024]{0:T(1024)S(1)} %copy-done.61), kind=kCustom, calls=%fused_computation | custom fusion | bytes 83888640 | tf_op jit(solution)/shard_map/jit(_take)/gather | solution.py:328
  994.1 28.6 %select_select_fusion = f32[16,40,16384]{2,1,0:T(8,128)} fusion(f32[16,40,16384]{2,1,0:T(8,128)} %bitcast.198, pred[16,40]{1,0:T(8,128)(4,1)S(1)} %copy-done.68, pred[16,40]{1,0:T(8,128)(4,1)S(1)} %copy-done.67), kind=kLoop, calls=%fused_computation.3 | loop fusion | flops 20971520 | bytes 83887360 | tf_op jit(solution)/shard_map/jit(_where)/select_n | solution.py:329
  1022.7 6.4 all-to-all-start
  1030.6 9.2 fusion.43
  1042.4 721.6 %all-to-all-done = f32[16,40,16384]{2,1,0:T(8,128)} async-done(((f32[16,40,16384]{2,1,0:T(8,128)}), f32[16,40,16384]{2,1,0:T(8,128)}, u32[]{:S(2)}, u32[]{:S(2)}) %all-to-all-start) | async-done | bytes 41943072 | tf_op jit(solution)/shard_map/all_to_all | solution.py:330
  1764.0 15.9 reduce_sum.256
  1784.5 207.8 %psum.15 = f32[8832]{0:T(1024)S(1)} all-reduce(f32[8832]{0:T(1024)S(1)} %constant_dynamic-update-slice_fusion.5), channel_id=1, replica_groups=mesh['seq'=2,'dp'=16] {'seq','dp'}, use_global_device_ids=true, to_apply=%region_28.29 | all-reduce | flops 8832 | bytes 70656 | tf_op jit(solution)/shard_map/psum | solution.py:327
  1993.0 28.9 %all-reduce.2.cloned.1.call-done = f32[40,16384]{1,0:T(8,128)} async-done(((f32[40,16384]{1,0:T(8,128)}), f32[40,16384]{1,0:T(8,128)}) %all-reduce.2.cloned.1.call-update) | async-done | bytes 2621456 | tf_op jit(solution)/shard_map/psum | solution.py:338
  2021.8 9.1 fusion.87
  (305 shorter events, 143.9 us)
Async XLA Ops:
  7.2 10.0 copy-start.2
  7.2 114.8 %all-gather.2.cloned.1.call-start = ((), (), s32[]{:S(2)}) async-start(), calls=%async_computation.1 | async-start | bytes 22282240 | tf_op jit(solution)/shard_map/all_gather | solution.py:181
  17.4 872.8 %copy-start.49 = (f32[512]{0:T(512)}, f32[512]{0:T(512)S(1)}, u32[]{:S(2)}) copy-start(f32[512]{0:T(512)S(1)} %broadcast_multiply_fusion.1) | copy-start | bytes 6148
  17.8 110.7 %copy-start.56 = (f32[512]{0:T(512)}, f32[512]{0:T(512)S(1)}, u32[]{:S(2)}) copy-start(f32[512]{0:T(512)S(1)} %fusion.33) | copy-start | bytes 6148
  17.8 872.4 %copy-start.54 = (f32[512]{0:T(512)}, f32[512]{0:T(512)S(1)}, u32[]{:S(2)}) copy-start(f32[512]{0:T(512)S(1)} %fusion.65) | copy-start | bytes 6148
  18.4 871.8 %copy-start.47 = (f32[768]{0:T(1024)}, f32[768]{0:T(1024)S(1)}, u32[]{:S(2)}) copy-start(f32[768]{0:T(1024)S(1)} %get-tuple-element.109) | copy-start | bytes 9220
  666.8 36.9 %collective-permute-start = (bf16[512,768]{0,1:T(8,128)(2,1)}, bf16[512,768]{0,1:T(8,128)(2,1)}, u32[]{:S(2)}, u32[]{:S(2)}) collective-permute-start(bf16[512,768]{0,1:T(8,128)(2,1)} %get-tuple-element.103), channel_id=1, source_target_pairs={{0,16},{16,0},{1,17},{17,1},{2,18},{18,2},{3,19},{19,3},{4,20},{20... | collective-permute-start | bytes 2359304 | tf_op jit(solution)/shard_map/ppermute | solution.py:25
  675.0 31.3 %collective-permute-start.1 = (bf16[512,768]{1,0:T(8,128)(2,1)}, bf16[512,768]{1,0:T(8,128)(2,1)}, u32[]{:S(2)}, u32[]{:S(2)}) collective-permute-start(bf16[512,768]{1,0:T(8,128)(2,1)} %convolution_convert_fusion.1), channel_id=1, source_target_pairs={{0,16},{16,0},{1,17},{17,1},{2,18},{18,2},{3,19},{19,3},{4,20},{20... | collective-permute-start | bytes 2359304 | tf_op jit(solution)/shard_map/ppermute | solution.py:25
  693.9 9.8 copy-start.22
  721.0 11.8 copy-start.41
  723.4 10.7 slice-start.11
  733.8 15.0 copy-start.12
  753.5 16.1 slice-start.3
  753.5 16.1 slice-start.4
  781.4 16.5 slice-start
  781.4 16.5 slice-start.1
  806.1 13.4 copy-start.31
  818.0 50.8 %collective-permute-start.3 = (f32[512,768]{1,0:T(8,128)}, f32[512,768]{1,0:T(8,128)}, u32[]{:S(2)}, u32[]{:S(2)}) collective-permute-start(f32[512,768]{1,0:T(8,128)} %slice_bitcast_fusion), channel_id=1, source_target_pairs={{0,16},{16,0},{1,17},{17,1},{2,18},{18,2},{3,19},{19,3},{4,20},{20... | collective-permute-start | bytes 4718600 | tf_op jit(solution)/shard_map/ppermute | solution.py:25
  829.6 58.4 %collective-permute-start.2 = (f32[512,768]{0,1:T(8,128)}, f32[512,768]{0,1:T(8,128)}, u32[]{:S(2)}, u32[]{:S(2)}) collective-permute-start(f32[512,768]{0,1:T(8,128)} %slice_bitcast_fusion.2), channel_id=1, source_target_pairs={{0,16},{16,0},{1,17},{17,1},{2,18},{18,2},{3,19},{19,3},{4,20},{20... | collective-permute-start | bytes 4718600 | tf_op jit(solution)/shard_map/ppermute | solution.py:25
  831.8 10.4 copy-start.27
  831.8 10.4 copy-start.42
  831.8 10.4 copy-start.44
  901.2 11.2 slice-start.6
  902.8 9.6 slice-start.8
  916.3 29.3 %copy-start.61 = (s32[1024]{0:T(1024)S(1)}, s32[1024]{0:T(1024)}, u32[]{:S(2)}) copy-start(s32[1024]{0:T(1024)} %pad_clamp_fusion) | copy-start | bytes 12292
  945.5 48.5 %copy-start.67 = (pred[16,40]{1,0:T(8,128)(4,1)S(1)}, pred[16,40]{1,0:T(8,128)(4,1)}, u32[]{:S(2)}) copy-start(pred[16,40]{1,0:T(8,128)(4,1)} %broadcast_in_dim.170) | copy-start | bytes 1924
  945.5 48.5 %copy-start.68 = (pred[16,40]{1,0:T(8,128)(4,1)S(1)}, pred[16,40]{1,0:T(8,128)(4,1)}, u32[]{:S(2)}) copy-start(pred[16,40]{1,0:T(8,128)(4,1)} %broadcast_in_dim.172) | copy-start | bytes 1924
  1022.7 741.3 %all-to-all-start = ((f32[16,40,16384]{2,1,0:T(8,128)}), f32[16,40,16384]{2,1,0:T(8,128)}, u32[]{:S(2)}, u32[]{:S(2)}) async-start(f32[16,40,16384]{2,1,0:T(8,128)} %select_select_fusion), calls=%async_computation | async-start | bytes 83886080 | tf_op jit(solution)/shard_map/all_to_all | solution.py:330
  1029.2 992.7 %all-reduce.2.cloned.1.call-start = ((), (), s32[]{:S(2)}) async-start(), calls=%async_computation.2 | async-start | bytes 5242880 | tf_op jit(solution)/shard_map/psum | solution.py:338
  1781.6 210.7 %copy-start.46 = (f32[8832]{0:T(1024)S(1)}, f32[8832]{0:T(1024)}, u32[]{:S(2)}) copy-start(f32[8832]{0:T(1024)} %param.19) | copy-start | bytes 105988
  1781.6 210.7 %copy-start.52 = (f32[8832]{0:T(1024)S(1)}, f32[8832]{0:T(1024)}, u32[]{:S(2)}) copy-start(f32[8832]{0:T(1024)} %param.20) | copy-start | bytes 105988
  1781.6 210.7 %copy-start.53 = (f32[8832]{0:T(1024)S(1)}, f32[8832]{0:T(1024)}, u32[]{:S(2)}) copy-start(f32[8832]{0:T(1024)} %param.21) | copy-start | bytes 105988
  (64 other events, 226.5 us)
Sparse Core Ops, SparseCore 0:
  10.4 111.5 all-gather.1
  1780.1 241.7 all-reduce.1
where the time goes:
time: 2050 us; the launch traced here: 2040 us
  waiting for transfers between devices  865 us (42%)
  local copies, waits for them, and re-layouts  730 us (36%)
  blocking collectives  208 us (10%)
  matrix products  113 us (6%)
  other arithmetic  95.7 us (5%)
    all_to_all x1, waiting for transfers between devices, shards(): lax.all_to_all(slot_term.reshape(dp_count, capacity, tile_len), 'dp', spl...  722 us
    scatter x1, local copies, waits for them, and re-layouts, shards(): tiles = jnp.zeros((tile_count, tile_len), jnp.bfloat16).at[owner_inverse]...  516 us
    psum x1, blocking collectives, shards(): vector_total = lax.psum(vector_grad, ('seq', 'dp'))  208 us
    all_gather x1, waiting for transfers between devices, shards(): lax.all_gather(masters.astype(jnp.bfloat16), 'dp', axis=0, tiled=True)  102 us
    gather x1, local copies, waits for them, and re-layouts, shards(): jnp.take(grad_tiles, jnp.minimum(owner_inverse, tile_count - 1), axis=0)  48.5 us
  transfers between devices with their start and end apart: 7, of which 4 were waited for; matrix products, arithmetic and copies ran while one was open for 6% of the time, Pallas kernels for 0%

commit v1 on v0

--- a/solution.py
+++ b/solution.py
@@ -174,12 +174,10 @@
     dp_count = lax.axis_size("dp")
     tile_count = owners.shape[0]
     slot_index = slot_numbers(owners)
-    owner_inverse = inverse_of(owners * capacity + slot_index, capacity * dp_count)
-    tiles = (
-        jnp.zeros((tile_count, tile_len), jnp.bfloat16)
-        .at[owner_inverse]
-        .set(lax.all_gather(masters.astype(jnp.bfloat16), "dp", axis=0, tiled=True), mode="drop")
-    )
+    slot_rows = owners * capacity + slot_index
+    owner_inverse = inverse_of(slot_rows, capacity * dp_count)
+    gathered = lax.all_gather(masters.astype(jnp.bfloat16), "dp", axis=0, tiled=True)
+    tiles = jnp.take(gathered, slot_rows, axis=0)
     w_query, w_key, w_value, w_out, w_up, w_down = split_weights(tiles.reshape(-1))
     (
         gain_one,
@@ -325,17 +323,11 @@
         ]
     )
     vector_total = lax.psum(vector_grad, ("seq", "dp"))
-    picked = jnp.take(grad_tiles, jnp.minimum(owner_inverse, tile_count - 1), axis=0)
-    slot_term = jnp.where((owner_inverse < tile_count)[:, None], picked, 0.0)
-    received = lax.all_to_all(
-        slot_term.reshape(dp_count, capacity, tile_len),
-        "dp",
-        split_axis=0,
-        concat_axis=0,
-        tiled=True,
-    )
-    owned_sum = jnp.sum(received, axis=0)
-    reduced = lax.psum(owned_sum, "seq")
+    grad_low = grad_tiles.astype(jnp.bfloat16)
+    picked = jnp.take(grad_low, jnp.minimum(owner_inverse, tile_count - 1), axis=0)
+    slot_term = jnp.where((owner_inverse < tile_count)[:, None], picked, jnp.zeros((), jnp.bfloat16))
+    owned_sum = lax.psum_scatter(slot_term, "dp", scatter_dimension=0, tiled=True)
+    reduced = lax.psum(owned_sum, "seq").astype(jnp.float32)
     new_master, new_one, new_two = adam_step(
         masters, moment_one, moment_two, reduced, RATE_MATRIX, DECAY_MATRIX
     )

time: 2050 us -> 814 us (0.40)
  waiting for transfers between devices: 865 us -> 318 us
  local copies, waits for them, and re-layouts: 730 us -> 233 us
  blocking collectives: 208 us -> 40.1 us
    all_to_all x1 -> x0, waiting for transfers between devices: 722 us -> none  [shards(): lax.all_to_all(slot_term.reshape(dp_count, capacity, tile_len), 'dp', spl...]
    scatter x1 -> x0, local copies, waits for them, and re-layouts: 516 us -> none  [shards(): tiles = jnp.zeros((tile_count, tile_len), jnp.bfloat16).at[owner_inverse]...]
    reduce_scatter x0 -> x1, waiting for transfers between devices: none -> 193 us  [shards(): lax.psum_scatter(slot_term, 'dp', scatter_dimension=0, tiled=True)]
    psum x1, blocking collectives: 208 us -> 40.1 us  [shards(): vector_total = lax.psum(vector_grad, ('seq', 'dp'))]
    gather x1 -> x2, local copies, waits for them, and re-layouts: 48.5 us -> 89.8 us  [the longest x1 47.5 us: shards(): jnp.take(grad_low, jnp.minimum(owner_inverse, tile_count - 1), axis=0)]
    reshape x1 -> x0, local copies, waits for them, and re-layouts: 29.3 us -> none  [shards(): grad_tiles = jnp.concatenate([grad_w_query.reshape(-1), grad_w_key.reshap...]
    psum x1, waiting for transfers between devices: 28.9 us -> 3.14 us  [shards(): reduced = lax.psum(owned_sum, 'seq').astype(jnp.float32)]
    convert_element_type x0 -> x1, local copies, waits for them, and re-layouts: none -> 20.9 us  [shards(): grad_low = grad_tiles.astype(jnp.bfloat16)]
  transfers between devices with their start and end apart: 7 -> 7, of which waited for: 4 -> 4; matrix products, arithmetic and copies ran while one was open for 6% -> 15% of each run, Pallas kernels for 0% -> 0%
where the time goes in v1:
time: 814 us; the launch traced here: 803 us
  waiting for transfers between devices  318 us (39%)
  local copies, waits for them, and re-layouts  233 us (29%)
  matrix products  114 us (14%)
  other arithmetic  79.1 us (10%)
  blocking collectives  40.1 us (5%)
  between operations  15.2 us (2%)
    reduce_scatter x1, waiting for transfers between devices, shards(): lax.psum_scatter(slot_term, 'dp', scatter_dimension=0, tiled=True)  193 us
    all_gather x1, waiting for transfers between devices, shards(): lax.all_gather(masters.astype(jnp.bfloat16), 'dp', axis=0, tiled=True)  104 us
    gather x1, local copies, waits for them, and re-layouts, shards(): jnp.take(grad_low, jnp.minimum(owner_inverse, tile_count - 1), axis=0)  47.5 us
    gather x1, local copies, waits for them, and re-layouts, shards(): tiles = jnp.take(gathered, slot_rows, axis=0)  42.3 us
    psum x1, blocking collectives, shards(): vector_total = lax.psum(vector_grad, ('seq', 'dp'))  40.1 us
    unnamed x198, local copies, waits for them, and re-layouts  32.8 us
    reshape x6, local copies, waits for them, and re-layouts, split_weights(): pieces.append(flat[offset:offset + length].reshape(matrix_shape))  31.2 us
    convert_element_type x1, local copies, waits for them, and re-layouts, shards(): grad_low = grad_tiles.astype(jnp.bfloat16)  20.9 us
  transfers between devices with their start and end apart: 7, of which 4 were waited for; matrix products, arithmetic and copies ran while one was open for 15% of the time, Pallas kernels for 0%

profile of v1, /device:TPU:0, one launch (start us, length us, event | category | flops | bytes accessed | tf_op | source)
XLA Modules:
  0.0 802.8 jit_solution(2855750141377509772)
XLA Ops:
  18.2 103.8 %all-gather.2.cloned.1.call-done = bf16[640,16384]{1,0:T(8,128)(2,1)} async-done(((bf16[40,16384]{1,0:T(8,128)(2,1)}), bf16[640,16384]{1,0:T(8,128)(2,1)}) %all-gather.2.cloned.1.call-update) | async-done | bytes 20971536 | tf_op jit(solution)/shard_map/all_gather | solution.py:179
  122.0 42.3 %gather_fusion = bf16[414,16384]{1,0:T(8,128)(2,1)} fusion(bf16[640,16384]{1,0:T(8,128)(2,1)} %all-gather.2.cloned.1.call-done, s32[1024]{0:T(1024)S(1)} %pad_clamp_fusion.1), kind=kCustom, calls=%fused_computation | custom fusion | bytes 27133560 | tf_op jit(solution)/shard_map/jit(_take)/gather | solution.py:180
  164.3 7.3 broadcast_select_fusion
  171.6 4.9 copy-done.2
  178.6 9.7 %fusion.86 = (bf16[144,16384]{1,0:T(8,128)(2,1)}, bf16[144,16384]{1,0:T(8,128)(2,1)}) fusion(bf16[414,16384]{1,0:T(8,128)(2,1)} %copy-done.2), kind=kLoop, calls=%fused_computation.194 | loop fusion | bytes 18874368 | tf_op jit(solution)/shard_map/slice | solution.py:55
  194.4 3.7 reshape.553
  201.8 3.7 reshape.551
  208.5 9.4 %reshape.563 = bf16[768,3072]{1,0:T(8,128)(2,1)} reshape(bf16[144,16384]{1,0:T(8,128)(2,1)} %get-tuple-element.87) | data formatting | bytes 9437184 | tf_op jit(solution)/shard_map/reshape | solution.py:55
  223.0 9.9 %reshape.564 = bf16[3072,768]{1,0:T(8,128)(2,1)} reshape(bf16[144,16384]{1,0:T(8,128)(2,1)} %get-tuple-element.88) | data formatting | bytes 9437184 | tf_op jit(solution)/shard_map/reshape | solution.py:55
  258.4 3.5 fusion.49
  266.2 8.2 %convert_reduce_fusion = (f32[3072]{0:T(1024)}, bf16[512,3072]{1,0:T(8,128)(2,1)S(1)}) fusion(bf16[3072,768]{1,0:T(8,128)(2,1)S(1)} %bitcast.208, bf16[1,512,768]{2,1,0:T(8,128)(2,1)S(1)} %copy-done.21, f32[512,3072]{1,0:T(8,128)S(1)} %fusion.75, f32[3072]{0:T(1024)S(1)} %copy-done.57), kind=kOutput, calls=%fused_computation.38 | convolution fusion | flops 2458383360 | bytes 14966784 | tf_op jit(solution)/shard_map/rd,fd->rf/dot_general | solution.py:235
  274.4 3.5 multiply_reduce_fusion.2
  282.8 7.8 fusion.12
  290.5 9.0 %multiply_reduce_fusion.1 = (f32[6,512]{1,0:T(8,128)S(1)}, f32[6,512,1024]{2,1,0:T(8,128)}) fusion(f32[6,512,1024]{2,1,0:T(8,128)} %copy-done.1, f32[6,512]{1,0:T(8,128)S(1)} %copy-done.35, bf16[512,6,64]{0,2,1:T(8,128)(2,1)S(1)} %bitcast.216, bf16[1024,6,64]{0,2,1:T(8,128)(2,1)S(1)} %bitcast.222), kind=kOutput, calls=%fused_computation.9 | convolution fusion | flops 412087296 | bytes 26370048 | tf_op jit(solution)/shard_map/while/body/eval_jaxpr/qhd,khd->hqk/dot_general | solution.py:131
  299.6 6.7 multiply_convert_fusion.1
  311.5 7.1 fusion.10
  318.6 9.0 %multiply_reduce_fusion = (f32[6,512]{1,0:T(8,128)S(1)}, f32[6,512,1024]{2,1,0:T(8,128)}) fusion(f32[6,512,1024]{2,1,0:T(8,128)} %copy-done, f32[6,512]{1,0:T(8,128)S(1)} %log_add_fusion, bf16[512,6,64]{0,2,1:T(8,128)(2,1)S(1)} %bitcast.218, bf16[1024,6,64]{0,2,1:T(8,128)(2,1)S(1)} %bitcast.220), kind=kOutput, calls=%fused_computation.6 | convolution fusion | flops 412087296 | bytes 26370048 | tf_op jit(solution)/shard_map/while/body/eval_jaxpr/qhd,khd->hqk/dot_general | solution.py:131
  327.6 6.2 multiply_convert_fusion
  353.7 3.5 reshape.581
  363.6 8.7 %convolution_convert_fusion = bf16[3072,768]{1,0:T(8,128)(2,1)} fusion(bf16[1,512,768]{2,1,0:T(8,128)(2,1)S(1)} %copy-done.22, f32[512,3072]{1,0:T(8,128)} %copy-done.75, f32[3072]{0:T(1024)S(1)} %copy-done.58), kind=kOutput, calls=%fused_computation.44 | convolution fusion | flops 2434007040 | bytes 11808768 | tf_op jit(solution)/shard_map/rf,rd->fd/dot_general | solution.py:231
  372.3 9.3 %reshape.586 = bf16[2359296]{0:T(1024)(128)(2,1)} reshape(bf16[3072,768]{1,0:T(8,128)(2,1)} %convolution_convert_fusion) | data formatting | bytes 9437184 | tf_op jit(solution)/shard_map/reshape | solution.py:309
  381.7 5.1 fusion.22
  386.8 3.6 copy.57
  402.5 17.6 %collective-permute-done.2 = f32[512,768]{0,1:T(8,128)} collective-permute-done((f32[512,768]{0,1:T(8,128)}, f32[512,768]{0,1:T(8,128)}, u32[]{:S(2)}, u32[]{:S(2)}) %collective-permute-start.2) | collective-permute-done | bytes 1572896 | tf_op jit(solution)/shard_map/ppermute | solution.py:25
  433.0 6.4 constant_dynamic-update-slice_fusion.1
  441.9 20.9 %convert_element_type.137 = bf16[414,16384]{1,0:T(8,128)(2,1)} reshape(bf16[6782976]{0:T(1024)(128)(2,1)} %constant_dynamic-update-slice_fusion) | data formatting | bytes 27131904 | tf_op jit(solution)/shard_map/convert_element_type | solution.py:326
  462.8 47.5 %gather_fusion.1 = bf16[640,16384]{1,0:T(8,128)(2,1)} fusion(bf16[414,16384]{1,0:T(8,128)(2,1)} %convert_element_type.137, s32[1024]{0:T(1024)S(1)} %copy-done.54), kind=kCustom, calls=%fused_computation.1 | custom fusion | bytes 41945600 | tf_op jit(solution)/shard_map/jit(_take)/gather | solution.py:327
  510.3 17.9 %select_select_fusion = bf16[640,16384]{1,0:T(8,128)(2,1)} fusion(bf16[640,16384]{1,0:T(8,128)(2,1)} %gather_fusion.1, pred[640]{0:T(1024)(128)(4,1)} %get-tuple-element.114, pred[640]{0:T(1024)(128)(4,1)} %get-tuple-element.113), kind=kLoop, calls=%fused_computation.3 | loop fusion | flops 20971520 | bytes 41944320 | tf_op jit(solution)/shard_map/jit(_where)/select_n | solution.py:328
  531.8 10.4 %fusion.44 = bf16[1,512,768]{2,1,0:T(8,128)(2,1)} fusion(f32[512,768]{1,0:T(8,128)S(1)} %copy-done.11, bf16[3072,768]{1,0:T(8,128)(2,1)} %reshape.564, f32[768]{0:T(1024)S(1)} %copy-done.62, f32[512,3072]{1,0:T(8,128)} %copy-done.75, f32[3072]{0:T(1024)S(1)} %copy-done.59), kind=kOutput, calls=%fused_computation.105 | convolution fusion | flops 2432827392 | bytes 13384704 | tf_op jit(solution)/shard_map/dot_general | solution.py:229
  546.1 193.0 %reduce-scatter.2.cloned.1.call-done = bf16[40,16384]{1,0:T(8,128)(2,1)} async-done(((bf16[640,16384]{1,0:T(8,128)(2,1)}), bf16[40,16384]{1,0:T(8,128)(2,1)}) %reduce-scatter.2.cloned.1.call-update) | async-done | bytes 1310736 | tf_op jit(solution)/shard_map/reduce_scatter | solution.py:329
  743.6 40.1 %psum.15 = f32[8832]{0:T(1024)S(1)} all-reduce(f32[8832]{0:T(1024)S(1)} %constant_dynamic-update-slice_fusion.5), channel_id=1, replica_groups=mesh['seq'=2,'dp'=16] {'seq','dp'}, use_global_device_ids=true, to_apply=%region_27.28 | all-reduce | flops 8832 | bytes 70656 | tf_op jit(solution)/shard_map/psum | solution.py:325
  787.5 8.5 %fusion.83 = (bf16[40,16384]{1,0:T(8,128)(2,1)}, f32[40,16384]{1,0:T(8,128)}, f32[40,16384]{1,0:T(8,128)}, f32[40,16384]{1,0:T(8,128)}) fusion(f32[40,16384]{1,0:T(8,128)} %param.16, bf16[40,16384]{1,0:T(8,128)(2,1)} %all-reduce.2.cloned.1.call-done, f32[40,16384]{1,0:T(8,128)} %param.17, f32[40,16384]{1,0:T(8,128)} %param.18), kind=kLoop, calls=%fused_computation.192 | loop fusion | flops 10485760 | bytes 18350080 | tf_op jit(solution)/shard_map/convert_element_type | solution.py:344
  (305 shorter events, 139.3 us)
Async XLA Ops:
  7.2 114.8 %all-gather.2.cloned.1.call-start = ((), (), s32[]{:S(2)}) async-start(), calls=%async_computation.1 | async-start | bytes 22282240 | tf_op jit(solution)/shard_map/all_gather | solution.py:179
  10.3 728.8 %reduce-scatter.2.cloned.1.call-start = ((), (), s32[]{:S(2)}) async-start(), calls=%async_computation.2 | async-start | bytes 22282240 | tf_op jit(solution)/shard_map/reduce_scatter | solution.py:329
  16.2 189.3 %copy-start.40 = (f32[512]{0:T(512)}, f32[512]{0:T(512)S(1)}, u32[]{:S(2)}) copy-start(f32[512]{0:T(512)S(1)} %broadcast_multiply_fusion.1) | copy-start | bytes 6148
  16.6 147.7 %copy-start.49 = (f32[512]{0:T(512)}, f32[512]{0:T(512)S(1)}, u32[]{:S(2)}) copy-start(f32[512]{0:T(512)S(1)} %fusion.34) | copy-start | bytes 6148
  16.6 188.9 %copy-start.45 = (f32[512]{0:T(512)}, f32[512]{0:T(512)S(1)}, u32[]{:S(2)}) copy-start(f32[512]{0:T(512)S(1)} %fusion.63) | copy-start | bytes 6148
  17.8 187.7 %copy-start.38 = (f32[768]{0:T(1024)}, f32[768]{0:T(1024)S(1)}, u32[]{:S(2)}) copy-start(f32[768]{0:T(1024)S(1)} %get-tuple-element.111) | copy-start | bytes 9220
  17.8 187.7 %copy-start.63 = (f32[768]{0:T(1024)}, f32[768]{0:T(1024)S(1)}, u32[]{:S(2)}) copy-start(f32[768]{0:T(1024)S(1)} %get-tuple-element.110) | copy-start | bytes 9220
  178.6 9.8 %slice-start.6 = ((bf16[414,16384]{1,0:T(8,128)(2,1)}), bf16[18,16384]{1,0:T(8,128)(2,1)S(1)}, s32[]{:S(2)}) async-start(bf16[414,16384]{1,0:T(8,128)(2,1)} %copy-done.2), calls=%async_computation.10 | async-start | bytes 1572864 | tf_op jit(solution)/shard_map/slice | solution.py:55
  192.9 39.9 %collective-permute-start = (bf16[512,768]{0,1:T(8,128)(2,1)}, bf16[512,768]{0,1:T(8,128)(2,1)}, u32[]{:S(2)}, u32[]{:S(2)}) collective-permute-start(bf16[512,768]{0,1:T(8,128)(2,1)} %get-tuple-element.105), channel_id=1, source_target_pairs={{0,16},{16,0},{1,17},{17,1},{2,18},{18,2},{3,19},{19,3},{4,20},{20... | collective-permute-start | bytes 2359304 | tf_op jit(solution)/shard_map/ppermute | solution.py:25
  201.2 34.3 %collective-permute-start.1 = (bf16[512,768]{1,0:T(8,128)(2,1)}, bf16[512,768]{1,0:T(8,128)(2,1)}, u32[]{:S(2)}, u32[]{:S(2)}) collective-permute-start(bf16[512,768]{1,0:T(8,128)(2,1)} %convolution_convert_fusion.6), channel_id=1, source_target_pairs={{0,16},{16,0},{1,17},{17,1},{2,18},{18,2},{3,19},{19,3},{4,20},{20... | collective-permute-start | bytes 2359304 | tf_op jit(solution)/shard_map/ppermute | solution.py:25
  223.0 16.7 %copy-start.14 = (bf16[512,384]{0,1:T(8,128)(2,1)}, bf16[512,384]{0,1:T(8,128)(2,1)S(1)}, u32[]{:S(2)}) copy-start(bf16[512,384]{0,1:T(8,128)(2,1)S(1)} %copy.48) | copy-start | bytes 1179652
  250.0 12.0 %copy-start.71 = (bf16[6,64,512]{2,1,0:T(8,128)(2,1)}, bf16[6,64,512]{2,1,0:T(8,128)(2,1)S(1)}, u32[]{:S(2)}) copy-start(bf16[6,64,512]{2,1,0:T(8,128)(2,1)S(1)} %fusion.48) | copy-start | bytes 1179652
  252.4 10.9 %slice-start.11 = ((s8[4718592]{0:T(1024)(128)(4,1)}), s8[4194304]{0:T(1024)(128)(4,1)S(1)}, s32[]{:S(2)}) async-start(s8[4718592]{0:T(1024)(128)(4,1)} %bitcast.209), calls=%async_computation.15 | async-start | bytes 8388608
  263.0 15.0 %copy-start.10 = (f32[512,768]{1,0:T(8,128)}, f32[512,768]{1,0:T(8,128)S(1)}, u32[]{:S(2)}) copy-start(f32[512,768]{1,0:T(8,128)S(1)} %get-tuple-element.124) | copy-start | bytes 4718596
  263.0 15.0 %copy-start.47 = (f32[512]{0:T(512)}, f32[512]{0:T(512)S(1)}, u32[]{:S(2)}) copy-start(f32[512]{0:T(512)S(1)} %broadcast_multiply_fusion) | copy-start | bytes 6148
  263.3 14.6 %copy-start.61 = (f32[512]{0:T(512)}, f32[512]{0:T(512)S(1)}, u32[]{:S(2)}) copy-start(f32[512]{0:T(512)S(1)} %fusion.64) | copy-start | bytes 6148
  282.7 16.8 %slice-start.3 = ((s8[12582912]{0:T(1024)(128)(4,1)}), s8[4194304]{0:T(1024)(128)(4,1)S(1)}, s32[]{:S(2)}) async-start(s8[12582912]{0:T(1024)(128)(4,1)} %bitcast.194), calls=%async_computation.7 | async-start | bytes 8388608
  282.7 16.8 %slice-start.4 = ((s8[12582912]{0:T(1024)(128)(4,1)}), s8[4194304]{0:T(1024)(128)(4,1)S(1)}, s32[]{:S(2)}) async-start(s8[12582912]{0:T(1024)(128)(4,1)} %bitcast.194), calls=%async_computation.8 | async-start | bytes 8388608
  311.5 16.1 %slice-start = ((s8[12582912]{0:T(1024)(128)(4,1)}), s8[4194304]{0:T(1024)(128)(4,1)S(1)}, s32[]{:S(2)}) async-start(s8[12582912]{0:T(1024)(128)(4,1)} %bitcast.192), calls=%async_computation.4 | async-start | bytes 8388608
  311.5 16.1 %slice-start.1 = ((s8[12582912]{0:T(1024)(128)(4,1)}), s8[4194304]{0:T(1024)(128)(4,1)S(1)}, s32[]{:S(2)}) async-start(s8[12582912]{0:T(1024)(128)(4,1)} %bitcast.192), calls=%async_computation.5 | async-start | bytes 8388608
  350.1 45.5 %collective-permute-start.3 = (f32[512,768]{1,0:T(8,128)}, f32[512,768]{1,0:T(8,128)}, u32[]{:S(2)}, u32[]{:S(2)}) collective-permute-start(f32[512,768]{1,0:T(8,128)} %slice_bitcast_fusion), channel_id=1, source_target_pairs={{0,16},{16,0},{1,17},{17,1},{2,18},{18,2},{3,19},{19,3},{4,20},{20... | collective-permute-start | bytes 4718600 | tf_op jit(solution)/shard_map/ppermute | solution.py:25
  361.9 58.2 %collective-permute-start.2 = (f32[512,768]{0,1:T(8,128)}, f32[512,768]{0,1:T(8,128)}, u32[]{:S(2)}, u32[]{:S(2)}) collective-permute-start(f32[512,768]{0,1:T(8,128)} %slice_bitcast_fusion.2), channel_id=1, source_target_pairs={{0,16},{16,0},{1,17},{17,1},{2,18},{18,2},{3,19},{19,3},{4,20},{20... | collective-permute-start | bytes 4718600 | tf_op jit(solution)/shard_map/ppermute | solution.py:25
  372.3 9.3 %copy-start.11 = (f32[512,768]{1,0:T(8,128)S(1)}, f32[512,768]{1,0:T(8,128)}, u32[]{:S(2)}) copy-start(f32[512,768]{1,0:T(8,128)} %copy-done.10) | copy-start | bytes 4718596
  372.3 9.3 %copy-start.48 = (f32[512]{0:T(512)S(1)}, f32[512]{0:T(512)}, u32[]{:S(2)}) copy-start(f32[512]{0:T(512)} %copy-done.47) | copy-start | bytes 6148
  441.9 20.9 %copy-start.54 = (s32[1024]{0:T(1024)S(1)}, s32[1024]{0:T(1024)}, u32[]{:S(2)}) copy-start(s32[1024]{0:T(1024)} %pad_clamp_fusion) | copy-start | bytes 12292
  528.3 259.3 %all-reduce.2.cloned.1.call-start = ((), (), s32[]{:S(2)}) async-start(), calls=%async_computation.3 | async-start | bytes 2621440 | tf_op jit(solution)/shard_map/psum | solution.py:330
  531.8 10.4 %copy-start.28 = (bf16[768,768]{1,0:T(8,128)(2,1)S(1)}, bf16[768,768]{1,0:T(8,128)(2,1)}, u32[]{:S(2)}) copy-start(bf16[768,768]{1,0:T(8,128)(2,1)} %reshape.553) | copy-start | bytes 3538948
  531.8 10.4 %copy-start.33 = (bf16[512,768]{0,1:T(8,128)(2,1)S(1)}, bf16[512,768]{0,1:T(8,128)(2,1)}, u32[]{:S(2)}) copy-start(bf16[512,768]{0,1:T(8,128)(2,1)} %copy-done.32) | copy-start | bytes 2359300
  545.2 193.9 %copy-start.53 = (f32[512]{0:T(512)S(1)}, f32[512]{0:T(512)}, u32[]{:S(2)}) copy-start(f32[512]{0:T(512)} %copy-done.52) | copy-start | bytes 6148
  739.1 44.6 %copy-start.37 = (f32[8832]{0:T(1024)S(1)}, f32[8832]{0:T(1024)}, u32[]{:S(2)}) copy-start(f32[8832]{0:T(1024)} %param.19) | copy-start | bytes 105988
  739.1 44.6 %copy-start.43 = (f32[8832]{0:T(1024)S(1)}, f32[8832]{0:T(1024)}, u32[]{:S(2)}) copy-start(f32[8832]{0:T(1024)} %param.20) | copy-start | bytes 105988
  739.2 44.6 %copy-start.44 = (f32[8832]{0:T(1024)S(1)}, f32[8832]{0:T(1024)}, u32[]{:S(2)}) copy-start(f32[8832]{0:T(1024)} %param.21) | copy-start | bytes 105988
  (65 other events, 229.6 us)
Sparse Core Ops, SparseCore 0:
  10.4 111.5 all-gather.1
  528.4 210.6 reduce-scatter.1
  741.4 46.1 all-reduce.1

commit v2 on v1

v2 whole, which is shorter than its diff:
```python
import functools

import jax
import jax.numpy as jnp
from jax import lax
from jax.experimental import pallas as pl
from jax.experimental.pallas import tpu as pltpu
from jax.sharding import PartitionSpec as P

D = 768
HD = 64
FF = 3072
STEP = 10
HV = 384
LANE = 128
QKV = 2 * D + HV
FF_STEP = 512
VEC = 7 * D + HV + FF
MIB = 1024 * 1024

EPS_NORM = 1e-05
EPS_ADAM = 1e-08
BETA_ONE = 0.5
BETA_TWO = 0.5
RATE_MATRIX = 0.03
RATE_VECTOR = 0.25
DECAY_MATRIX = 0.1
FAR = -1e30

BF16 = jnp.bfloat16
F32 = jnp.float32

NN = (((1,), (0,)), ((), ()))
NT = (((1,), (1,)), ((), ()))
TN = (((0,), (0,)), ((), ()))


def mm(left, right, dims=NN):
    return lax.dot_general(left, right, dims, preferred_element_type=F32)


def vec_part(vec_ref, index):
    if index < 7:
        return vec_ref[:, index * D : (index + 1) * D]
    if index == 7:
        return vec_ref[:, 7 * D : 7 * D + HV]
    return vec_ref[:, 7 * D + HV :]


def params(mib, **more):
    return pltpu.CompilerParams(vmem_limit_bytes=mib * MIB, **more)


def whole(shape):
    return pl.BlockSpec(shape, lambda *_: (0,) * len(shape))


def cost(flops, bytes_accessed, transcendentals=0):
    return pl.CostEstimate(
        flops=int(flops), bytes_accessed=int(bytes_accessed), transcendentals=int(transcendentals)
    )


def adam_step(weight, first_moment, second_moment, gradient, step_rate, weight_decay):
    first_new = BETA_ONE * first_moment + (1.0 - BETA_ONE) * gradient
    second_new = BETA_TWO * second_moment + (1.0 - BETA_TWO) * gradient * gradient
    first_fix = 1.0 - BETA_ONE**STEP
    second_fix = 1.0 - BETA_TWO**STEP
    update = first_new / first_fix / (jnp.sqrt(second_new / second_fix) + EPS_ADAM)
    return (weight - step_rate * (update + weight_decay * weight), first_new, second_new)


def slot_numbers(owners):
    tile_order = jnp.arange(owners.shape[0], dtype=jnp.int32)
    earlier = (owners[None, :] == owners[:, None]) & (tile_order[None, :] < tile_order[:, None])
    return jnp.sum(earlier.astype(jnp.int32), axis=1)


def normed(values):
    center = jnp.mean(values, axis=-1, keepdims=True)
    centred = values - center
    spread = jnp.mean(centred * centred, axis=-1, keepdims=True)
    rate = lax.rsqrt(spread + EPS_NORM)
    return centred * rate, rate


def norm_back(grad, hat, rate, gain):
    g = grad * gain
    return rate * (
        g - jnp.mean(g, axis=-1, keepdims=True) - hat * jnp.mean(g * hat, axis=-1, keepdims=True)
    )


def pack_kernel(src, dst, flat):
    rows = src.shape[0]
    for c in range(LANE):
        flat[pl.ds(c, rows, stride=LANE), :] = src[:, c * LANE : (c + 1) * LANE]
    dst[...] = flat[...].astype(BF16)


def pack_slots(masters):
    capacity, tile_len = masters.shape
    rows = 8 if capacity % 8 == 0 else capacity
    return pl.pallas_call(
        pack_kernel,
        out_shape=jax.ShapeDtypeStruct((capacity * LANE, LANE), BF16),
        grid=(capacity // rows,),
        in_specs=[pl.BlockSpec((rows, tile_len), lambda i: (i, 0))],
        out_specs=pl.BlockSpec((rows * LANE, LANE), lambda i: (i, 0)),
        scratch_shapes=[pltpu.VMEM((rows * LANE, LANE), F32)],
        compiler_params=params(32),
        cost_estimate=cost(0, capacity * tile_len * 6),
        name="pack_slots",
    )(masters)


def weight_chunks():
    chunks = [
        (0, 36, 6, 0, 0, 0),
        (36, 36, 6, 0, D, 0),
        (72, 18, 3, 0, 2 * D, 0),
        (90, 36, 6, 1, 0, 0),
    ]
    for i in range(4):
        chunks.append((126 + 36 * i, 36, 24, 2, 0, 192 * i))
    for i in range(4):
        chunks.append((270 + 36 * i, 36, 6, 3, 0, 768 * i))
    return chunks


def unpack_kernel(slot_rows, slots, w_qkv, w_out, w_up, w_down, stage, o_qkv, o_out, o_up, o_down, flat, sems, out_sems):
    chunks = weight_chunks()
    places = (o_qkv, o_out, o_up, o_down)
    ends = (w_qkv, w_out, w_up, w_down)

    for number, (first, tiles, _, _, _, _) in enumerate(chunks):

        @pl.loop(0, tiles)
        def _(i, first=first, number=number):
            t = first + i
            pltpu.make_async_copy(
                slots.at[pl.ds(pl.multiple_of(slot_rows[t] * LANE, LANE), LANE)],
                stage.at[pl.ds(pl.multiple_of(t * LANE, LANE), LANE)],
                sems.at[number],
            ).start()

    copies = []
    for number, (first, tiles, per_row, matrix, column, row) in enumerate(chunks):
        span = pl.ds(first * LANE, tiles * LANE)
        pltpu.make_async_copy(stage.at[span], stage.at[span], sems.at[number]).wait()
        place = places[matrix]
        lines = 3 * LANE // per_row

        @pl.loop(0, tiles // 6)
        def _(g, first=first, per_row=per_row, place=place, column=column, row=row, lines=lines):
            for half in range(2):
                base = pl.multiple_of(first * LANE + (2 * g + half) * 3 * LANE, LANE)
                flat[half] = stage[pl.ds(base, 3 * LANE), :].astype(F32)
            for half in range(2):
                top = pl.multiple_of(row + (2 * g + half) * lines, 16)
                for j in range(per_row):
                    place[pl.ds(top, lines), column + j * LANE : column + (j + 1) * LANE] = flat[
                        half, pl.ds(j, lines, stride=per_row), :
                    ].astype(BF16)

        rows = tiles * LANE // per_row
        columns = pl.ds(column, per_row * LANE)
        copy = pltpu.make_async_copy(
            place.at[pl.ds(row, rows), columns],
            ends[matrix].at[pl.ds(row, rows), columns],
            out_sems.at[number],
        )
        copy.start()
        copies.append(copy)
    for copy in copies:
        copy.wait()


def unpack_weights(slot_rows, slots):
    tile_count = slot_rows.shape[0]
    shapes = [(D, QKV), (D, D), (D, FF), (FF, D)]
    any_space = pl.BlockSpec(memory_space=pl.ANY)
    return pl.pallas_call(
        unpack_kernel,
        out_shape=[jax.ShapeDtypeStruct(s, BF16) for s in shapes],
        grid_spec=pltpu.PrefetchScalarGridSpec(
            num_scalar_prefetch=1,
            grid=(1,),
            in_specs=[any_space],
            out_specs=[any_space] * 4,
            scratch_shapes=[pltpu.VMEM((tile_count * LANE, LANE), BF16)]
            + [pltpu.VMEM(s, BF16) for s in shapes]
            + [
                pltpu.VMEM((2, 3 * LANE, LANE), F32),
                pltpu.SemaphoreType.DMA((12,)),
                pltpu.SemaphoreType.DMA((12,)),
            ],
        ),
        compiler_params=params(48),
        cost_estimate=cost(0, 4 * tile_count * LANE * LANE),
        name="unpack_weights",
    )(slot_rows, slots)


def project_kernel(tokens, firsts, w_qkv, vec, n1, q, k, v):
    hat, _ = normed(tokens[...].astype(F32))
    low = (hat * vec_part(vec, 0) + vec_part(vec, 1)).astype(BF16)
    n1[...] = low

    @pl.when(pl.program_id(0) < 2)
    def _():
        query = mm(low, w_qkv[:, :D]) + vec_part(vec, 4)
        q[...] = (query.astype(BF16).astype(F32) * HD ** (-0.5)).astype(BF16)

    k[...] = mm(low, w_qkv[:, D : 2 * D]).astype(BF16)
    v[:, :HV] = (mm(low, w_qkv[:, 2 * D :]) + vec_part(vec, 7)).astype(BF16)
    v[:, HV:] = firsts[...]


def project(tokens, firsts, w_qkv, vec):
    rows = tokens.shape[0]
    step = rows // 4
    by_row = lambda i: (i, 0)
    return pl.pallas_call(
        project_kernel,
        out_shape=[
            jax.ShapeDtypeStruct((rows, D), BF16),
            jax.ShapeDtypeStruct((rows // 2, D), BF16),
            jax.ShapeDtypeStruct((rows, D), BF16),
            jax.ShapeDtypeStruct((rows, D), BF16),
        ],
        grid=(4,),
        in_specs=[
            pl.BlockSpec((step, D), by_row),
            pl.BlockSpec((step, HV), by_row),
            whole((D, QKV)),
            whole((1, VEC)),
        ],
        out_specs=[
            pl.BlockSpec((step, D), by_row),
            pl.BlockSpec((step, D), lambda i: (jnp.minimum(i, 1), 0)),
            pl.BlockSpec((step, D), by_row),
            pl.BlockSpec((step, D), by_row),
        ],
        compiler_params=params(48),
        cost_estimate=cost(2 * rows * D * QKV, 2 * D * QKV + rows * D * 10),
        name="project",
    )(tokens, firsts, w_qkv, vec)


def attend_kernel(q, k, v, row_pos, column_pos, out, chance, bias):
    queries = q.shape[0]
    block = queries // 2

    @pl.when(pl.program_id(0) == 0)
    def _():
        bias[...] = jnp.where(column_pos[...] <= row_pos[...], 0.0, FAR)

    for head in range(2):
        cols = slice(head * HD, (head + 1) * HD)
        key = k[:, cols]
        value = v[:, cols]
        for part in range(2):
            near = slice(part * block, (part + 1) * block)
            scores = mm(key, q[near, cols], NT) + bias[:, near]
            top = jnp.max(scores, axis=0, keepdims=True)
            power = jnp.exp(scores - top)
            total = jnp.sum(power, axis=0, keepdims=True)
            weights = (power * (1.0 / total)).astype(BF16)
            chance[head, :, near] = weights
            mixed = mm(value, weights, TN)
            out[near, cols] = mixed.T.astype(BF16)


def attend(q, k, v, row_pos, column_pos):
    queries, keys = q.shape[0], k.shape[0]
    pairs = D // LANE
    by_column = lambda i: (0, i)
    return pl.pallas_call(
        attend_kernel,
        out_shape=[
            jax.ShapeDtypeStruct((queries, D), BF16),
            jax.ShapeDtypeStruct((2 * pairs, keys, queries), BF16),
        ],
        grid=(pairs,),
        in_specs=[
            pl.BlockSpec((queries, LANE), by_column),
            pl.BlockSpec((keys, LANE), by_column),
            pl.BlockSpec((keys, LANE), by_column),
            whole((1, queries)),
            whole((keys, 1)),
        ],
        out_specs=[
            pl.BlockSpec((queries, LANE), by_column),
            pl.BlockSpec((2, keys, queries), lambda i: (i, 0, 0)),
        ],
        scratch_shapes=[pltpu.VMEM((keys, queries), F32)],
        compiler_params=params(48),
        cost_estimate=cost(4 * queries * keys * D, 24 * queries * keys, 12 * queries * keys),
        name="attend",
    )(q, k, v, row_pos, column_pos)


def hidden_kernel(
    tokens, att, og, w_out, w_up, w_down, vec,
    result, grad_resid, resid_low, grad_att, d_up, d_down, vec_grad,
    resid, hat, n2, rate, acc, acc_grad, flat_up, flat_down,
):
    step = pl.program_id(0)
    per_row = D // LANE
    wide = FF // LANE

    @pl.when(step == 0)
    def _():
        base = tokens[...].astype(F32) + mm(att[...], w_out[...]) + vec_part(vec, 5)
        resid[...] = base
        unit, scale = normed(base)
        hat[...] = unit
        rate[...] = scale
        n2[...] = (unit * vec_part(vec, 2) + vec_part(vec, 3)).astype(BF16)
        vec_grad[...] = jnp.zeros_like(vec_grad)

    start = pl.multiple_of(7 * D + HV + step * FF_STEP, LANE)
    pre = mm(n2[...], w_up[...]) + vec[:, pl.ds(start, FF_STEP)]
    square = pre * pre
    bent = jnp.tanh(0.7978845608028654 * (pre + 0.044715 * square * pre))
    half = 0.5 * (1.0 + bent)
    act = (pre * half).astype(BF16)
    slope = half + (0.5 * 0.7978845608028654) * pre * (1.0 - bent * bent) * (1.0 + 0.134145 * square)
    grad_pre32 = mm(og[...], w_down[...], NT) * slope
    grad_pre = grad_pre32.astype(BF16)
    vec_grad[:, pl.ds(start, FF_STEP)] = jnp.sum(grad_pre.astype(F32), axis=0, keepdims=True)
    more = mm(act, w_down[...])
    more_grad = mm(grad_pre, w_up[...], NT)

    @pl.when(step == 0)
    def _():
        acc[...] = more
        acc_grad[...] = more_grad

    @pl.when(step > 0)
    def _():
        acc[...] += more
        acc_grad[...] += more_grad

    down = mm(act, og[...], TN)
    for j in range(per_row):
        flat_down[pl.ds(j, FF_STEP, stride=per_row), :] = down[:, j * LANE : (j + 1) * LANE]
    d_down[...] = flat_down[...].astype(BF16)
    up = mm(n2[...], grad_pre, TN)
    for j in range(FF_STEP // LANE):
        flat_up[pl.ds(step * (FF_STEP // LANE) + j, D, stride=wide), :] = up[
            :, j * LANE : (j + 1) * LANE
        ]

    @pl.when(step == FF // FF_STEP - 1)
    def _():
        d_up[...] = flat_up[...].astype(BF16)
        result[...] = (resid[...] + acc[...] + vec_part(vec, 6)).astype(BF16)
        grad = acc_grad[...]
        unit = hat[...]
        vec_grad[:, 2 * D : 3 * D] = jnp.sum(grad * unit, axis=0, keepdims=True)
        vec_grad[:, 3 * D : 4 * D] = jnp.sum(grad, axis=0, keepdims=True)
        given = og[...].astype(F32)
        back = given + norm_back(grad, unit, rate[...], vec_part(vec, 2))
        grad_resid[...] = back
        low = back.astype(BF16)
        resid_low[...] = low
        vec_grad[:, 5 * D : 6 * D] = jnp.sum(low.astype(F32), axis=0, keepdims=True)
        vec_grad[:, 6 * D : 7 * D] = jnp.sum(given, axis=0, keepdims=True)
        grad_att[...] = mm(low, w_out[...], NT).astype(BF16)


def hidden(tokens, att, og, w_out, w_up, w_down, vec):
    rows = tokens.shape[0]
    line = (rows, D)
    flat_rows = FF * D // LANE
    return pl.pallas_call(
        hidden_kernel,
        out_shape=[
            jax.ShapeDtypeStruct(line, BF16),
            jax.ShapeDtypeStruct(line, F32),
            jax.ShapeDtypeStruct(line, BF16),
            jax.ShapeDtypeStruct(line, BF16),
            jax.ShapeDtypeStruct((flat_rows, LANE), BF16),
            jax.ShapeDtypeStruct((flat_rows, LANE), BF16),
            jax.ShapeDtypeStruct((1, VEC), F32),
        ],
        grid=(FF // FF_STEP,),
        in_specs=[
            whole(line),
            whole(line),
            whole(line),
            whole((D, D)),
            pl.BlockSpec((D, FF_STEP), lambda i: (0, i)),
            pl.BlockSpec((FF_STEP, D), lambda i: (i, 0)),
            whole((1, VEC)),
        ],
        out_specs=[
            whole(line),
            whole(line),
            whole(line),
            whole(line),
            whole((flat_rows, LANE)),
            pl.BlockSpec((FF_STEP * D // LANE, LANE), lambda i: (i, 0)),
            whole((1, VEC)),
        ],
        scratch_shapes=[
            pltpu.VMEM(line, F32),
            pltpu.VMEM(line, F32),
            pltpu.VMEM(line, BF16),
            pltpu.VMEM((rows, 1), F32),
            pltpu.VMEM(line, F32),
            pltpu.VMEM(line, F32),
            pltpu.VMEM((flat_rows, LANE), F32),
            pltpu.VMEM((FF_STEP * D // LANE, LANE), F32),
        ],
        compiler_params=params(58),
        cost_estimate=cost(2 * rows * D * (6 * FF + 2 * D), 8 * D * FF + 20 * rows * D, rows * FF),
        name="hidden",
    )(tokens, att, og, w_out, w_up, w_down, vec)


def attend_back_kernel(q, k, v, att, grad_att, chance, d_q, d_k, d_fresh, d_first):
    pair = pl.program_id(0)
    for head in range(2):
        cols = slice(head * HD, (head + 1) * HD)
        grad = grad_att[:, cols]
        weights = chance[head]
        shared = grad.astype(F32) * att[:, cols].astype(F32)
        delta = jnp.sum(shared.T, axis=0, keepdims=True)
        grad_chance = mm(v[:, cols], grad, NT)
        grad_scores = (weights.astype(F32) * (grad_chance - delta)).astype(BF16)
        grad_value = mm(weights, grad)

        @pl.when(pair < 3)
        def _(grad_value=grad_value, cols=cols):
            d_fresh[:, cols] = grad_value.astype(BF16)

        @pl.when(pair >= 3)
        def _(grad_value=grad_value, cols=cols):
            d_first[:, cols] = grad_value

        d_k[:, cols] = mm(grad_scores, q[:, cols]).astype(BF16)
        d_q[:, cols] = (mm(k[:, cols], grad_scores, TN).T * HD ** (-0.5)).astype(BF16)


def attend_back(q, k, v, att, grad_att, chance):
    queries, keys = q.shape[0], k.shape[0]
    pairs = D // LANE
    by_column = lambda i: (0, i)
    return pl.pallas_call(
        attend_back_kernel,
        out_shape=[
            jax.ShapeDtypeStruct((queries, D), BF16),
            jax.ShapeDtypeStruct((keys, D), BF16),
            jax.ShapeDtypeStruct((keys, HV), BF16),
            jax.ShapeDtypeStruct((keys, HV), F32),
        ],
        grid=(pairs,),
        in_specs=[
            pl.BlockSpec((queries, LANE), by_column),
            pl.BlockSpec((keys, LANE), by_column),
            pl.BlockSpec((keys, LANE), by_column),
            pl.BlockSpec((queries, LANE), by_column),
            pl.BlockSpec((queries, LANE), by_column),
            pl.BlockSpec((2, keys, queries), lambda i: (i, 0, 0)),
        ],
        out_specs=[
            pl.BlockSpec((queries, LANE), by_column),
            pl.BlockSpec((keys, LANE), by_column),
            pl.BlockSpec((keys, LANE), lambda i: (0, jnp.minimum(i, 2))),
            pl.BlockSpec((keys, LANE), lambda i: (0, jnp.maximum(i - 3, 0))),
        ],
        compiler_params=params(48),
        cost_estimate=cost(8 * queries * keys * D, 24 * queries * keys),
        name="attend_back",
    )(q, k, v, att, grad_att, chance)


def project_back_kernel(
    tokens, n1, d_q, d_k, d_fresh, att, resid_low, w_qkv, vec,
    grad_near, grad_far, d_rest, vec_grad, flat,
):
    rows = n1.shape[0] // 2
    per_row = D // LANE
    grads = mm(d_k[...], w_qkv[:, D : 2 * D], NT) + mm(d_fresh[...], w_qkv[:, 2 * D :], NT)
    near = grads[:rows] + mm(d_q[...], w_qkv[:, :D], NT)
    far = grads[rows:]
    grad_near[...] = near
    grad_far[...] = far.astype(BF16)
    hat, _ = normed(tokens[...].astype(F32))
    vec_grad[...] = jnp.zeros_like(vec_grad)
    vec_grad[:, :D] = jnp.sum(near * hat[:rows], axis=0, keepdims=True) + jnp.sum(
        far * hat[rows:], axis=0, keepdims=True
    )
    vec_grad[:, D : 2 * D] = jnp.sum(near, axis=0, keepdims=True) + jnp.sum(
        far, axis=0, keepdims=True
    )
    vec_grad[:, 4 * D : 5 * D] = jnp.sum(d_q[...].astype(F32), axis=0, keepdims=True)
    vec_grad[:, 7 * D : 7 * D + HV] = jnp.sum(d_fresh[...].astype(F32), axis=0, keepdims=True)
    pieces = (
        (n1, d_q, rows, 0, per_row),
        (n1, d_k, 2 * rows, D * per_row, per_row),
        (n1, d_fresh, 2 * rows, 2 * D * per_row, HV // LANE),
        (att, resid_low, rows, 2 * D * per_row + D * HV // LANE, per_row),
    )
    for left, right, count, start, columns in pieces:
        product = mm(left[:count], right[:count], TN)
        size = D * columns
        for j in range(columns):
            flat[pl.ds(j, D, stride=columns), :] = product[:, j * LANE : (j + 1) * LANE]
        d_rest[start : start + size] = flat[:size].astype(BF16)
    used = 3 * D * per_row + D * HV // LANE
    d_rest[used:] = jnp.zeros((d_rest.shape[0] - used, LANE), BF16)


def project_back(tokens, n1, d_q, d_k, d_fresh, att, resid_low, w_qkv, vec):
    rows = n1.shape[0] // 2
    vm = pl.BlockSpec(memory_space=pltpu.VMEM)
    return pl.pallas_call(
        project_back_kernel,
        out_shape=[
            jax.ShapeDtypeStruct((rows, D), F32),
            jax.ShapeDtypeStruct((rows, D), BF16),
            jax.ShapeDtypeStruct((128 * LANE, LANE), BF16),
            jax.ShapeDtypeStruct((1, VEC), F32),
        ],
        in_specs=[vm] * 9,
        out_specs=[vm] * 4,
        scratch_shapes=[pltpu.VMEM((D * D // LANE, LANE), F32)],
        compiler_params=params(58),
        cost_estimate=cost(2 * rows * D * (7 * D), 14 * MIB),
        name="project_back",
    )(tokens, n1, d_q, d_k, d_fresh, att, resid_low, w_qkv, vec)


def adam_kernel(places, grads, used, weight, one, two, new, new_one, new_two, low, stage, flat, sems):
    step = pl.program_id(0)
    rows = weight.shape[0]
    steps = pl.num_programs(0)

    @pl.when(step == 0)
    def _():
        @pl.loop(0, steps)
        def _(s):
            @pl.loop(0, rows)
            def _(i):
                slot = s * rows + i
                pltpu.make_async_copy(
                    grads.at[pl.ds(pl.multiple_of(places[slot] * LANE, LANE), LANE)],
                    stage.at[pl.ds(pl.multiple_of(slot * LANE, LANE), LANE)],
                    sems.at[s],
                ).start()

    span = pl.ds(pl.multiple_of(step * rows * LANE, LANE), rows * LANE)
    pltpu.make_async_copy(stage.at[span], stage.at[span], sems.at[step]).wait()
    flat[...] = stage[span, :].astype(F32)
    keep = used[...] > 0.0
    for c in range(LANE):
        columns = slice(c * LANE, (c + 1) * LANE)
        gradient = jnp.where(keep, flat[pl.ds(c, rows, stride=LANE), :], 0.0)
        after, after_one, after_two = adam_step(
            weight[:, columns], one[:, columns], two[:, columns], gradient, RATE_MATRIX, DECAY_MATRIX
        )
        new[:, columns] = after
        new_one[:, columns] = after_one
        new_two[:, columns] = after_two
        low[:, columns] = after.astype(BF16)


def adam(places, grads, used, weight, one, two):
    capacity, tile_len = weight.shape
    rows = 8 if capacity % 8 == 0 else capacity
    steps = capacity // rows
    block = pl.BlockSpec((rows, tile_len), lambda i, *_: (i, 0))
    return pl.pallas_call(
        adam_kernel,
        out_shape=[jax.ShapeDtypeStruct(weight.shape, F32)] * 3
        + [jax.ShapeDtypeStruct(weight.shape, BF16)],
        grid_spec=pltpu.PrefetchScalarGridSpec(
            num_scalar_prefetch=1,
            grid=(steps,),
            in_specs=[
                pl.BlockSpec(memory_space=pl.ANY),
                pl.BlockSpec((rows, LANE), lambda i, *_: (i, 0)),
                block,
                block,
                block,
            ],
            out_specs=[block] * 4,
            scratch_shapes=[
                pltpu.VMEM((capacity * LANE, LANE), BF16),
                pltpu.VMEM((rows * LANE, LANE), F32),
                pltpu.SemaphoreType.DMA((steps,)),
            ],
        ),
        compiler_params=params(48),
        cost_estimate=cost(20 * capacity * tile_len, 28 * capacity * tile_len, 2 * capacity * tile_len),
        name="adam",
    )(places, grads, used, weight, one, two)


def swap(value):
    return lax.ppermute(value, "seq", [(0, 1), (1, 0)])


def shards(
    tokens,
    first_values,
    out_grad,
    block_place,
    owners,
    masters,
    moment_one,
    moment_two,
    vector_master,
    vector_moment_one,
    vector_moment_two,
):
    capacity = masters.shape[0]
    dp_count = lax.axis_size("dp")
    tile_count = owners.shape[0]
    dp_here = lax.axis_index("dp")
    seq_here = lax.axis_index("seq")
    _, half_len, _ = tokens.shape

    tokens = tokens.reshape(half_len, D)
    firsts = first_values.reshape(half_len, HV)
    given = out_grad.reshape(half_len, D)
    tokens_far, firsts_far = swap(tokens), swap(firsts)
    packed = pack_slots(masters)
    slots = lax.all_gather(packed, "dp", axis=0, tiled=True)

    slot_index = slot_numbers(owners)
    slot_rows = owners * capacity + slot_index
    mine = (owners == dp_here)[None, :] & (
        slot_index[None, :] == jnp.arange(capacity, dtype=jnp.int32)[:, None]
    )
    tile_order = jnp.arange(tile_count, dtype=jnp.int32)
    tile_here = jnp.sum(jnp.where(mine, tile_order[None, :], 0), axis=1)
    tile_here = tile_here + jnp.where(tile_here >= 126, 2, 0)
    used = jnp.broadcast_to(
        jnp.any(mine, axis=1).astype(F32)[:, None], (capacity, LANE)
    )

    blocks = block_place.reshape(-1)
    per_device = blocks.shape[0] // 2
    block_len = half_len // per_device
    ordered = jnp.roll(blocks, -seq_here * per_device)
    all_pos = (
        ordered[:, None] * block_len + jnp.arange(block_len, dtype=jnp.int32)[None, :]
    ).reshape(-1)
    row_pos = all_pos[:half_len].reshape(1, half_len)
    column_pos = all_pos.reshape(2 * half_len, 1)

    vec = vector_master.reshape(1, VEC)
    tokens_all = jnp.concatenate([tokens, tokens_far], axis=0)
    firsts_all = jnp.concatenate([firsts, firsts_far], axis=0)

    w_qkv, w_out, w_up, w_down = unpack_weights(slot_rows, slots)
    n1, q, k, v = project(tokens_all, firsts_all, w_qkv, vec)
    att, chance = attend(q, k, v, row_pos, column_pos)
    result, grad_resid, resid_low, grad_att, d_up, d_down, vec_one = hidden(
        tokens, att, given, w_out, w_up, w_down, vec
    )
    d_q, d_k, d_fresh, d_first = attend_back(q, k, v, att, grad_att, chance)
    grad_near, grad_far, d_rest, vec_two = project_back(
        tokens_all, n1, d_q, d_k, d_fresh, att, resid_low, w_qkv, vec
    )
    grad_back = swap(grad_far)
    first_back = swap(d_first[half_len:].astype(BF16))
    both = ("seq", "dp")
    grads = lax.psum(jnp.concatenate([d_rest, d_up, d_down], axis=0), both)
    vector_total = lax.psum((vec_one + vec_two).reshape(VEC), both)

    grad_n1 = grad_near + grad_back.astype(F32)
    hat, rate = normed(tokens.astype(F32))
    tokens_grad = grad_resid + norm_back(grad_n1, hat, rate, vec[:, :D])
    first_grad = d_first[:half_len] + first_back.astype(F32)

    new_master, new_one, new_two, new_low = adam(
        tile_here, grads, used, masters, moment_one, moment_two
    )
    vector_new, vector_one, vector_two = adam_step(
        vector_master, vector_moment_one, vector_moment_two, vector_total, RATE_VECTOR, 0.0
    )
    return (
        result.reshape(1, half_len, D),
        tokens_grad.reshape(1, half_len, D),
        first_grad.reshape(1, half_len, HV),
        new_master,
        new_one,
        new_two,
        new_low,
        vector_new,
        vector_one,
        vector_two,
    )


def solution(mesh):
    rows = P("dp", "seq", None)
    slots = P("dp", None)
    return jax.shard_map(
        shards,
        mesh=mesh,
        in_specs=(rows, rows, rows, slots, P(), slots, slots, slots, P(), P(), P()),
        out_specs=(rows, rows, rows, slots, slots, slots, slots, P(), P(), P()),
        check_vma=False,
    )
```

time: 814 us -> 551 us (0.68); the launches traced: 803 us -> 550 us
  local copies, waits for them, and re-layouts: 233 us -> 17 us
  Pallas kernels: 0 us -> 125 us
  matrix products: 114 us -> 0 us
  waiting for transfers between devices: 318 us -> 259 us
  blocking collectives: 40.1 us -> 78.1 us
  other arithmetic: 79.1 us -> 51.3 us
    reduce_scatter x1 -> x0, waiting for transfers between devices: 193 us -> none  [shards(): lax.psum_scatter(slot_term, 'dp', scatter_dimension=0, tiled=True)]
    psum x1, waiting for transfers between devices: 3.14 us -> 154 us  [shards(): grads = lax.psum(jnp.concatenate([d_rest, d_up, d_down], axis=0), both)]
    pallas_call x0 -> x8, Pallas kernels: none -> 125 us  [the longest x1 31.5 us: hidden(): pl.pallas_call(hidden_kernel, out_shape=[jax.ShapeDtypeStruct(line, BF16)...]
    dot_general x30 -> x0, matrix products: 114 us -> none  [the longest x2 18 us: attend_back(): jnp.einsum('qhd,khd->hqk', grad_part, value_part, preferred_element_type=...]
    gather x2 -> x0, local copies, waits for them, and re-layouts: 89.8 us -> none  [the longest x1 47.5 us: shards(): jnp.take(grad_low, jnp.minimum(owner_inverse, tile_count - 1), axis=0)]
    reshape x15 -> x1, local copies, waits for them, and re-layouts: 61.4 us -> 0.03 us  [shards(): vec = vector_master.reshape(1, VEC)]
    concatenate x1 -> x4, other arithmetic: 0.01 us -> 40.6 us  [the longest x1 38.2 us: shards(): grads = lax.psum(jnp.concatenate([d_rest, d_up, d_down], axis=0), both)]
    psum x1, blocking collectives: 40.1 us -> 78.1 us  [shards(): vector_total = lax.psum((vec_one + vec_two).reshape(VEC), both)]
  transfers between devices with their start and end apart: 7 -> 6, of which waited for: 4 -> 3; matrix products, arithmetic and copies ran while one was open for 15% -> 3% of each run, Pallas kernels for 0% -> 0%
where the time goes in v2:
time: 551 us; the launch traced here: 550 us
  waiting for transfers between devices  259 us (47%)
  Pallas kernels  125 us (23%)
  blocking collectives  78.1 us (14%)
  other arithmetic  51.3 us (9%)
  local copies, waits for them, and re-layouts  17 us (3%)
  between operations  14.3 us (3%)
    psum x1, waiting for transfers between devices, shards(): grads = lax.psum(jnp.concatenate([d_rest, d_up, d_down], axis=0), both)  154 us
    all_gather x1, waiting for transfers between devices, shards(): slots = lax.all_gather(packed, 'dp', axis=0, tiled=True)  80.2 us
    psum x1, blocking collectives, shards(): vector_total = lax.psum((vec_one + vec_two).reshape(VEC), both)  78.1 us
    concatenate x1, other arithmetic, shards(): grads = lax.psum(jnp.concatenate([d_rest, d_up, d_down], axis=0), both)  38.2 us
    pallas_call x1, Pallas kernels, hidden(): pl.pallas_call(hidden_kernel, out_shape=[jax.ShapeDtypeStruct(line, BF16)...  31.5 us
    ppermute x4, waiting for transfers between devices, swap(): return lax.ppermute(value, 'seq', [(0, 1), (1, 0)])  25.2 us
    pallas_call x1, Pallas kernels, attend(): pl.pallas_call(attend_kernel, out_shape=[jax.ShapeDtypeStruct((queries, D...  25.2 us
    pallas_call x1, Pallas kernels, attend_back(): pl.pallas_call(attend_back_kernel, out_shape=[jax.ShapeDtypeStruct((queri...  24.5 us
  transfers between devices with their start and end apart: 6, of which 3 were waited for; matrix products, arithmetic and copies ran while one was open for 3% of the time, Pallas kernels for 0%

profile of v2, /device:TPU:0, one launch (start us, length us, event | category | flops | bytes accessed | tf_op | source)
XLA Modules:
  0.0 549.7 jit_solution(13539885276167077807)
XLA Ops:
  7.2 1.7 copy-done
  9.0 3.1 pack_slots.1
  12.1 3.0 collective-permute-start
  16.0 25.2 %collective-permute-done.1 = bf16[512,384]{1,0:T(8,128)(2,1)} collective-permute-done((bf16[512,384]{1,0:T(8,128)(2,1)S(1)}, bf16[512,384]{1,0:T(8,128)(2,1)}, u32[]{:S(2)}, u32[]{:S(2)}) %collective-permute-start.1) | collective-permute-done | bytes 393248 | tf_op jit(solution)/shard_map/ppermute | solution.py:605
  41.2 1.1 pad_maximum_fusion.2.firsts
  42.3 1.2 pad_maximum_fusion.1.tokens
  43.6 80.2 %all-gather.2.cloned.1.call-done.slots = bf16[81920,128]{1,0:T(8,128)(2,1)} async-done(((bf16[5120,128]{1,0:T(8,128)(2,1)}), bf16[81920,128]{1,0:T(8,128)(2,1)}) %all-gather.2.cloned.1.call-update) | async-done | bytes 20971536 | tf_op jit(solution)/shard_map/all_gather | solution.py:633
  123.8 10.3 %unpack_weights.1 = (bf16[768,1920]{1,0:T(8,128)(2,1)S(1)}, bf16[768,768]{1,0:T(8,128)(2,1)S(1)}, bf16[768,3072]{1,0:T(8,128)(2,1)}, bf16[3072,768]{1,0:T(8,128)(2,1)}) custom-call(s32[414]{0:T(512)S(1)} %multiply_add_fusion.1.slot_rows, bf16[81920,128]{1,0:T(8,128)(2,1)} %all-gather.2.cloned.1.call-done.slots), custom_call_target="tpu_custom_call" | custom-call | bytes 27131904 | tf_op jit(solution)/shard_map/unpack_weights/pallas_call | solution.py:183
  134.1 1.6 copy-done.9
  135.6 8.3 %project.1 = (bf16[1024,768]{1,0:T(8,128)(2,1)S(1)}, bf16[512,768]{1,0:T(8,128)(2,1)S(1)}, bf16[1024,768]{1,0:T(8,128)(2,1)S(1)}, bf16[1024,768]{1,0:T(8,128)(2,1)}) custom-call(bf16[1024,768]{1,0:T(8,128)(2,1)} %pad_maximum_fusion.1.tokens, bf16[1024,384]{1,0:T(8,128)(2,1)S(1)} %pad_maximum_fusion.2.firsts, bf16[768,1920]{1,0:T(8,128)(2,1)} %copy-done.9, ...), custom_call_target="tpu_custom_call" | custom-call | flops 3019898880 | bytes 10813440 | tf_op jit(solution)/shard_map/project/pallas_call | solution.py:224
  144.0 1.1 copy-done.14
  145.1 2.0 copy-done.4
  147.1 25.2 %attend.1 = (bf16[512,768]{1,0:T(8,128)(2,1)S(1)}, bf16[12,1024,512]{2,1,0:T(8,128)(2,1)}) custom-call(bf16[512,768]{1,0:T(8,128)(2,1)S(1)} %get-tuple-element.40.q, bf16[1024,768]{1,0:T(8,128)(2,1)S(1)} %get-tuple-element.41.k, bf16[1024,768]{1,0:T(8,128)(2,1)S(1)} %copy-done.4, s32[1,512]{1,0:T(1,128)S(1)} %bitcast.23, s32[1024,1]{1,0:T(8,128)S(1)} %bitcast.22), custom_call_target="tpu_custom_call" | custom-call | flops 1610612736 | bytes 12582912 | tf_op jit(solution)/shard_map/attend/pallas_call | solution.py:279
  172.3 0.9 copy-done.5
  173.1 31.5 %hidden.1 = (bf16[512,768]{1,0:T(8,128)(2,1)}, f32[512,768]{1,0:T(8,128)}, bf16[512,768]{1,0:T(8,128)(2,1)}, bf16[512,768]{1,0:T(8,128)(2,1)}, bf16[18432,128]{1...) custom-call(bf16[512,768]{1,0:T(8,128)(2,1)} %bitcast.24, bf16[512,768]{1,0:T(8,128)(2,1)} %copy-done.5, ...), custom_call_target="tpu_custom_call" | custom-call | flops 15703474176 | bytes 26738688 | tf_op jit(solution)/shard_map/hidden/pallas_call | solution.py:378
  204.6 1.1 copy-done.7
  205.8 24.5 %attend_back.1 = (bf16[512,768]{1,0:T(8,128)(2,1)S(1)}, bf16[1024,768]{1,0:T(8,128)(2,1)S(1)}, bf16[1024,384]{1,0:T(8,128)(2,1)S(1)}, f32[1024,384]{1,0:T(8,128)}) custom-call(bf16[512,768]{1,0:T(8,128)(2,1)S(1)} %get-tuple-element.40.q, bf16[1024,768]{1,0:T(8,128)(2,1)} %copy-done.3, bf16[1024,768]{1,0:T(8,128)(2,1)} %get-tuple-element.42.v, ...), custom_call_target="tpu_custom_call" | custom-call | flops 3221225472 | bytes 12582912 | tf_op jit(solution)/shard_map/attend_back/pallas_call | solution.py:452
  230.3 1.1 copy-done.10
  231.4 0.9 copy-done.12
  232.3 0.9 copy-done.13
  233.2 13.0 %project_back.1 = (f32[512,768]{1,0:T(8,128)}, bf16[512,768]{1,0:T(8,128)(2,1)}, bf16[16384,128]{1,0:T(8,128)(2,1)}, f32[1,8832]{1,0:T(1,128)}) custom-call(bf16[1024,768]{1,0:T(8,128)(2,1)} %pad_maximum_fusion.1.tokens, bf16[1024,768]{1,0:T(8,128)(2,1)} %copy-done.14, bf16[512,768]{1,0:T(8,128)(2,1)} %copy-done.12, bf16[1024,768]{1,0:T(8,128)(2,1)} %copy-done.10, ...), custom_call_target="tpu_custom_call" | custom-call | flops 4227858432 | bytes 14680064 | tf_op jit(solution)/shard_map/project_back/pallas_call | solution.py:521
  246.2 38.2 %pad_maximum_fusion = bf16[53248,128]{1,0:T(8,128)(2,1)} fusion(bf16[18432,128]{1,0:T(8,128)(2,1)} %get-tuple-element.61, bf16[18432,128]{1,0:T(8,128)(2,1)S(1)} %bitcast.28, bf16[16384,128]{1,0:T(8,128)(2,1)} %get-tuple-element.59), kind=kLoop, calls=%fused_computation | loop fusion | flops 40894464 | bytes 27262976 | tf_op jit(solution)/shard_map/concatenate | solution.py:674
  286.5 1.3 slice.25
  287.8 1.5 collective-permute-start.3
  289.9 1.5 add_reduce_fusion
  291.4 78.1 %psum.15 = f32[8832]{0:T(1024)} all-reduce(f32[8832]{0:T(1024)} %add_reduce_fusion), channel_id=1, replica_groups=mesh['seq'=2,'dp'=16] {'seq','dp'}, use_global_device_ids=true, to_apply=%region_8.9 | all-reduce | flops 8832 | bytes 70656 | tf_op jit(solution)/shard_map/psum | solution.py:675
  369.5 1.5 multiply_subtract_fusion
  371.0 2.2 add_bitcast_fusion
  375.4 3.1 fusion.8
  378.5 153.7 %all-reduce.2.cloned.1.call-done.grads = bf16[53248,128]{1,0:T(8,128)(2,1)} async-done(((bf16[53248,128]{1,0:T(8,128)(2,1)}), bf16[53248,128]{1,0:T(8,128)(2,1)}) %all-reduce.2.cloned.1.call-update) | async-done | bytes 13631504 | tf_op jit(solution)/shard_map/psum | solution.py:674
  532.2 1.7 copy-done.2
  534.0 8.9 %adam.1 = (f32[40,16384]{1,0:T(8,128)}, f32[40,16384]{1,0:T(8,128)}, f32[40,16384]{1,0:T(8,128)}, bf16[40,16384]{1,0:T(8,128)(2,1)}) custom-call(s32[40]{0:T(128)S(1)} %fusion.16.places, bf16[53248,128]{1,0:T(8,128)(2,1)} %all-reduce.2.cloned.1.call-done.grads, f32[40,128]{1,0:T(8,128)S(1)} %broadcast_in_dim.26.used, f32[40,16384]{1,0:T(8,128)S(1)} %copy-done.1, ...), custom_call_target="tpu_custom_call" | custom-call | flops 13107200 | bytes 18350080 | tf_op jit(solution)/shard_map/adam/pallas_call | solution.py:577
  (79 shorter events, 5.8 us)
Async XLA Ops:
  7.2 116.6 %all-gather.2.cloned.1.call-start = ((), (), s32[]{:S(2)}) async-start(), calls=%async_computation | async-start | bytes 22282240 | tf_op jit(solution)/shard_map/all_gather | solution.py:633
  7.2 1.7 copy-start
  9.0 3.1 copy-start.15
  9.0 6.2 %copy-start.21 = (bf16[1,512,384]{2,1,0:T(8,128)(2,1)S(1)}, bf16[1,512,384]{2,1,0:T(8,128)(2,1)}, u32[]{:S(2)}) copy-start(bf16[1,512,384]{2,1,0:T(8,128)(2,1)} %param.12) | copy-start | bytes 1179652
  9.0 6.3 %copy-start.25 = (s32[1,4]{1,0:T(1,128)S(1)}, s32[1,4]{1,0:T(1,128)}, u32[]{:S(2)}) copy-start(s32[1,4]{1,0:T(1,128)} %param.14) | copy-start | bytes 52
  12.0 3.7 copy-start.22
  12.0 3.7 copy-start.23
  12.1 520.1 %all-reduce.2.cloned.1.call-start = ((), (), s32[]{:S(2)}) async-start(), calls=%async_computation.1 | async-start | bytes 27262976 | tf_op jit(solution)/shard_map/psum | solution.py:674
  12.1 30.2 %collective-permute-start = (bf16[512,768]{1,0:T(8,128)(2,1)S(1)}, bf16[512,768]{1,0:T(8,128)(2,1)S(1)}, u32[]{:S(2)}, u32[]{:S(2)}) collective-permute-start(bf16[512,768]{1,0:T(8,128)(2,1)S(1)} %bitcast.25), channel_id=1, source_target_pairs={{0,16},{16,0},{1,17},{17,1},{2,18},{18,2},{3,19},{19,3},{4,20},{20... | collective-permute-start | bytes 2359304 | tf_op jit(solution)/shard_map/ppermute | solution.py:605
  15.2 26.1 %collective-permute-start.1 = (bf16[512,384]{1,0:T(8,128)(2,1)S(1)}, bf16[512,384]{1,0:T(8,128)(2,1)}, u32[]{:S(2)}, u32[]{:S(2)}) collective-permute-start(bf16[512,384]{1,0:T(8,128)(2,1)S(1)} %bitcast.29), channel_id=1, source_target_pairs={{0,16},{16,0},{1,17},{17,1},{2,18},{18,2},{3,19},{19,3},{4,20},{20... | collective-permute-start | bytes 1179656 | tf_op jit(solution)/shard_map/ppermute | solution.py:605
  15.8 119.9 %copy-start.8 = (f32[1,8832]{1,0:T(1,128)}, f32[1,8832]{1,0:T(1,128)S(1)}, u32[]{:S(2)}) copy-start(f32[1,8832]{1,0:T(1,128)S(1)} %reshape.106.vec) | copy-start | bytes 105988
  134.0 1.6 copy-start.9
  135.6 8.3 %copy-start.11 = (bf16[768,768]{1,0:T(8,128)(2,1)}, bf16[768,768]{1,0:T(8,128)(2,1)S(1)}, u32[]{:S(2)}) copy-start(bf16[768,768]{1,0:T(8,128)(2,1)S(1)} %get-tuple-element.44.w_out) | copy-start | bytes 3538948
  144.0 1.1 copy-start.14
  145.1 27.1 %copy-start.3 = (bf16[1024,768]{1,0:T(8,128)(2,1)}, bf16[1024,768]{1,0:T(8,128)(2,1)S(1)}, u32[]{:S(2)}) copy-start(bf16[1024,768]{1,0:T(8,128)(2,1)S(1)} %get-tuple-element.41.k) | copy-start | bytes 4718596
  145.1 2.0 copy-start.4
  173.1 31.5 %copy-start.6 = (bf16[512,768]{1,0:T(8,128)(2,1)S(1)}, bf16[512,768]{1,0:T(8,128)(2,1)}, u32[]{:S(2)}) copy-start(bf16[512,768]{1,0:T(8,128)(2,1)} %copy-done.5) | copy-start | bytes 2359300
  204.6 1.1 copy-start.7
  230.3 1.1 copy-start.10
  232.3 0.9 copy-start.13
  233.2 13.0 %slice-start = ((s8[4718592]{0:T(1024)(128)(4,1)}), s8[4194304]{0:T(1024)(128)(4,1)S(1)}, s32[]{:S(2)}) async-start(s8[4718592]{0:T(1024)(128)(4,1)} %bitcast.27), calls=%async_computation.2 | async-start | bytes 8388608
  233.2 13.0 %slice-start.1 = ((s8[4718592]{0:T(1024)(128)(4,1)}), s8[524288]{0:T(1024)(128)(4,1)S(1)}, s32[]{:S(2)}) async-start(s8[4718592]{0:T(1024)(128)(4,1)} %bitcast.27), calls=%async_computation.3 | async-start | bytes 1048576
  284.4 1.5 copy-start.16
  286.5 86.7 %copy-start.17 = (f32[512,768]{1,0:T(8,128)S(1)}, f32[512,768]{1,0:T(8,128)}, u32[]{:S(2)}) copy-start(f32[512,768]{1,0:T(8,128)} %get-tuple-element.56) | copy-start | bytes 4718596
  287.8 83.2 %collective-permute-start.3 = (bf16[512,384]{1,0:T(8,128)(2,1)S(1)}, bf16[512,384]{1,0:T(8,128)(2,1)}, u32[]{:S(2)}, u32[]{:S(2)}) collective-permute-start(bf16[512,384]{1,0:T(8,128)(2,1)S(1)} %slice.25), channel_id=1, source_target_pairs={{0,16},{16,0},{1,17},{17,1},{2,18},{18,2},{3,19},{19,3},{4,20},{20... | collective-permute-start | bytes 1179656 | tf_op jit(solution)/shard_map/ppermute | solution.py:605
  289.4 83.9 %collective-permute-start.2 = (bf16[512,768]{1,0:T(8,128)(2,1)}, bf16[512,768]{1,0:T(8,128)(2,1)S(1)}, u32[]{:S(2)}, u32[]{:S(2)}) collective-permute-start(bf16[512,768]{1,0:T(8,128)(2,1)} %get-tuple-element.57), channel_id=1, source_target_pairs={{0,16},{16,0},{1,17},{17,1},{2,18},{18,2},{3,19},{19,3},{4,20},{20... | collective-permute-start | bytes 2359304 | tf_op jit(solution)/shard_map/ppermute | solution.py:605
  373.3 0.9 copy-start.19
  373.3 1.7 copy-start.18
  373.3 2.2 copy-start.20
  375.4 156.7 %copy-start.24 = (f32[40]{0:T(128)S(1)}, f32[40]{0:T(128)}, u32[]{:S(2)}) copy-start(f32[40]{0:T(128)} %convert_element_type.24) | copy-start | bytes 484
  375.4 156.8 %copy-start.1 = (f32[40,16384]{1,0:T(8,128)S(1)}, f32[40,16384]{1,0:T(8,128)}, u32[]{:S(2)}) copy-start(f32[40,16384]{1,0:T(8,128)} %weight.1) | copy-start | bytes 7864324
  532.2 1.7 copy-start.2
  (2 other events, 1.8 us)
Sparse Core Ops, SparseCore 0:
  12.2 111.5 all-gather.1
  284.6 247.5 all-reduce.1

commit v3 on v2

--- a/solution.py
+++ b/solution.py
@@ -17,6 +17,8 @@
 FF_STEP = 512
 VEC = 7 * D + HV + FF
 MIB = 1024 * 1024
+LINE = 4
+REST = 126 * LANE
 
 EPS_NORM = 1e-05
 EPS_ADAM = 1e-08
@@ -479,7 +481,7 @@
 
 
 def project_back_kernel(
-    tokens, n1, d_q, d_k, d_fresh, att, resid_low, w_qkv, vec,
+    tokens, n1, d_q, d_k, d_fresh, att, resid_low, w_qkv, vec, vec_one,
     grad_near, grad_far, d_rest, vec_grad, flat,
 ):
     rows = n1.shape[0] // 2
@@ -490,7 +492,7 @@
     grad_near[...] = near
     grad_far[...] = far.astype(BF16)
     hat, _ = normed(tokens[...].astype(F32))
-    vec_grad[...] = jnp.zeros_like(vec_grad)
+    vec_grad[...] = vec_one[...]
     vec_grad[:, :D] = jnp.sum(near * hat[:rows], axis=0, keepdims=True) + jnp.sum(
         far * hat[rows:], axis=0, keepdims=True
     )
@@ -511,11 +513,13 @@
         for j in range(columns):
             flat[pl.ds(j, D, stride=columns), :] = product[:, j * LANE : (j + 1) * LANE]
         d_rest[start : start + size] = flat[:size].astype(BF16)
-    used = 3 * D * per_row + D * HV // LANE
-    d_rest[used:] = jnp.zeros((d_rest.shape[0] - used, LANE), BF16)
-
-
-def project_back(tokens, n1, d_q, d_k, d_fresh, att, resid_low, w_qkv, vec):
+    flat[: 2 * LANE] = jnp.zeros((2 * LANE, LANE), F32)
+    for j in range(VEC // LANE):
+        flat[j : j + 1] = vec_grad[:, j * LANE : (j + 1) * LANE]
+    d_rest[REST:] = flat[: 2 * LANE].astype(BF16)
+
+
+def project_back(tokens, n1, d_q, d_k, d_fresh, att, resid_low, w_qkv, vec, vec_one):
     rows = n1.shape[0] // 2
     vm = pl.BlockSpec(memory_space=pltpu.VMEM)
     return pl.pallas_call(
@@ -524,15 +528,14 @@
             jax.ShapeDtypeStruct((rows, D), F32),
             jax.ShapeDtypeStruct((rows, D), BF16),
             jax.ShapeDtypeStruct((128 * LANE, LANE), BF16),
-            jax.ShapeDtypeStruct((1, VEC), F32),
-        ],
-        in_specs=[vm] * 9,
-        out_specs=[vm] * 4,
-        scratch_shapes=[pltpu.VMEM((D * D // LANE, LANE), F32)],
+        ],
+        in_specs=[vm] * 10,
+        out_specs=[vm] * 3,
+        scratch_shapes=[pltpu.VMEM((1, VEC), F32), pltpu.VMEM((D * D // LANE, LANE), F32)],
         compiler_params=params(58),
         cost_estimate=cost(2 * rows * D * (7 * D), 14 * MIB),
         name="project_back",
-    )(tokens, n1, d_q, d_k, d_fresh, att, resid_low, w_qkv, vec)
+    )(tokens, n1, d_q, d_k, d_fresh, att, resid_low, w_qkv, vec, vec_one)
 
 
 def adam_kernel(places, grads, used, weight, one, two, new, new_one, new_two, low, stage, flat, sems):
@@ -601,6 +604,448 @@
     )(places, grads, used, weight, one, two)
 
 
+RS_KINDS = ("core", "xa", "yb", "ya", "xb", "up", "down")
+AG_KINDS = ("g_up", "g_down", "g_xa", "g_yb", "g_ya", "g_xb", "g_ya2", "g_xb2", "g_c", "g_c2", "g_c3")
+
+
+class Links:
+    def __init__(self, line, send_sems, recv_sems):
+        dp = lax.axis_index("dp")
+        self.line = line
+        self.y = lax.axis_index("seq")
+        self.z = dp // 4
+        self.x = (dp // 2) % 2
+        self.c = dp % 2
+        self.send_sems, self.recv_sems = send_sems, recv_sems
+        self.to = {
+            "core": {"dp": self.z * 4 + self.x * 2 + (1 - self.c)},
+            "x": {"dp": self.z * 4 + (1 - self.x) * 2 + self.c},
+            "y": {"seq": 1 - self.y},
+            "up": {"dp": dp + 4},
+            "down": {"dp": dp - 4},
+        }
+        self.sent = []
+
+    def greet(self):
+        barrier = pltpu.get_barrier_semaphore()
+        for name in ("core", "x", "y"):
+            pl.semaphore_signal(barrier, inc=1, device_id=self.to[name])
+
+        @pl.when(self.z > 0)
+        def _():
+            pl.semaphore_signal(barrier, inc=1, device_id=self.to["down"])
+
+        @pl.when(self.z < self.line - 1)
+        def _():
+            pl.semaphore_signal(barrier, inc=1, device_id=self.to["up"])
+
+        pl.semaphore_wait(
+            barrier,
+            3 + jnp.where(self.z > 0, 1, 0) + jnp.where(self.z < self.line - 1, 1, 0),
+        )
+
+    def copy(self, source, target, index, way):
+        return pltpu.make_async_remote_copy(
+            src_ref=source,
+            dst_ref=target,
+            send_sem=self.send_sems.at[index],
+            recv_sem=self.recv_sems.at[index],
+            device_id=self.to[way],
+        )
+
+    def send(self, source, target, index, way, when=None):
+        if when is None:
+            self.copy(source, target, index, way).start()
+        else:
+
+            @pl.when(when)
+            def _():
+                self.copy(source, target, index, way).start()
+
+        self.sent.append((source, target, index, way, when))
+
+    def arrive(self, target, index, way):
+        self.copy(target, target, index, way).wait_recv()
+
+    def finish(self):
+        for source, target, index, way, when in self.sent:
+            if when is None:
+                self.copy(source, target, index, way).wait_send()
+            else:
+
+                @pl.when(when)
+                def _(source=source, target=target, index=index, way=way):
+                    self.copy(source, target, index, way).wait_send()
+
+
+def add_into(place, *others):
+    total = place[...].astype(F32)
+    for other in others:
+        total = total + other[...].astype(F32)
+    place[...] = total.astype(BF16)
+
+
+class Scatter:
+    def __init__(self, links, base, source, offset, rows, held, r_core, r_xa, r_yb, r_ya, r_xb, r_up, r_down, load_sems):
+        self.k, self.base, self.source, self.offset, self.rows = links, base, source, offset, rows
+        self.held, self.r_core = held, r_core
+        self.r_xa, self.r_yb, self.r_ya, self.r_xb = r_xa, r_yb, r_ya, r_xb
+        self.r_up, self.r_down, self.load_sems = r_up, r_down, load_sems
+        self.halves = (pl.ds(0, rows // 2), pl.ds(rows // 2, rows // 2))
+        order = []
+        low, high = 0, links.line - 1
+        while low <= high:
+            order.append(high)
+            if low < high:
+                order.append(low)
+            low, high = low + 1, high - 1
+        self.order = order
+
+    def at(self, kind, z):
+        return self.base + RS_KINDS.index(kind) * self.k.line + z
+
+    def load(self, z):
+        four = 4 * self.rows
+        start = self.offset + (self.k.c * self.k.line + z) * four
+        out = []
+        for i in range(4):
+            out.append(
+                pltpu.make_async_copy(
+                    self.source.at[pl.ds(pl.multiple_of(start + i * self.rows, 16), self.rows)],
+                    self.held.at[z, i // 2, i % 2],
+                    self.load_sems.at[4 * z + i],
+                )
+            )
+        return out
+
+    def begin(self):
+        k = self.k
+        for z in self.order:
+            start = self.offset + ((1 - k.c) * k.line + z) * 4 * self.rows
+            k.send(
+                self.source.at[pl.ds(pl.multiple_of(start, 16), 4 * self.rows)],
+                self.r_core.at[z],
+                self.at("core", z),
+                "core",
+            )
+            for copy in self.load(z):
+                copy.start()
+
+    def first(self, z):
+        k, (a, b) = self.k, self.halves
+        for copy in self.load(z):
+            copy.wait()
+        k.arrive(self.r_core.at[z], self.at("core", z), "core")
+        for i in range(4):
+            add_into(self.held.at[z, i // 2, i % 2], self.r_core.at[z, pl.ds(i * self.rows, self.rows)])
+        k.send(self.held.at[z, 1 - k.x, :, a], self.r_xa.at[z], self.at("xa", z), "x")
+        k.send(self.held.at[z, :, 1 - k.y, b], self.r_yb.at[z], self.at("yb", z), "y")
+
+    def second(self, z):
+        k, (a, b) = self.k, self.halves
+        k.arrive(self.r_xa.at[z], self.at("xa", z), "x")
+        for y in range(2):
+            add_into(self.held.at[z, k.x, y, a], self.r_xa.at[z, y])
+        k.send(self.held.at[z, k.x, 1 - k.y, a], self.r_ya.at[z], self.at("ya", z), "y")
+        k.arrive(self.r_yb.at[z], self.at("yb", z), "y")
+        for x in range(2):
+            add_into(self.held.at[z, x, k.y, b], self.r_yb.at[z, x])
+        k.send(self.held.at[z, 1 - k.x, k.y, b], self.r_xb.at[z], self.at("xb", z), "x")
+
+    def third(self, z):
+        k, (a, b) = self.k, self.halves
+        k.arrive(self.r_ya.at[z], self.at("ya", z), "y")
+        add_into(self.held.at[z, k.x, k.y, a], self.r_ya.at[z])
+        k.arrive(self.r_xb.at[z], self.at("xb", z), "x")
+        add_into(self.held.at[z, k.x, k.y, b], self.r_xb.at[z])
+        mine = self.held.at[z, k.x, k.y]
+
+        @pl.when((k.z < z) & (k.z > 0))
+        def _():
+            k.arrive(self.r_up.at[z], self.at("up", z), "up")
+            add_into(mine, self.r_up.at[z])
+
+        @pl.when((k.z > z) & (k.z < k.line - 1))
+        def _():
+            k.arrive(self.r_down.at[z], self.at("down", z), "down")
+            add_into(mine, self.r_down.at[z])
+
+        k.send(mine, self.r_up.at[z], self.at("up", z), "up", k.z < z)
+        k.send(mine, self.r_down.at[z], self.at("down", z), "down", k.z > z)
+
+    def last(self):
+        k = self.k
+        mine = self.held.at[k.z, k.x, k.y]
+
+        @pl.when(k.z > 0)
+        def _():
+            k.arrive(self.r_up.at[k.z], self.at("up", k.z), "up")
+            add_into(mine, self.r_up.at[k.z])
+
+        @pl.when(k.z < k.line - 1)
+        def _():
+            k.arrive(self.r_down.at[k.z], self.at("down", k.z), "down")
+            add_into(mine, self.r_down.at[k.z])
+
+
+class Gather:
+    def __init__(self, links, base, piece, out, rows, index, copy_sem):
+        self.k, self.base, self.piece, self.out, self.rows = links, base, piece, out, rows
+        self.index, self.copy_sem = index, copy_sem
+        self.halves = (pl.ds(0, rows // 2), pl.ds(rows // 2, rows // 2))
+
+    def at(self, kind, z):
+        return self.base + AG_KINDS.index(kind) * self.k.line + z
+
+    def spot(self, c, z, x, y, half=None):
+        start = self.index(c, z, x, y)
+        if half is None:
+            return self.out.at[pl.ds(pl.multiple_of(start, 16), self.rows)]
+        return self.out.at[pl.ds(pl.multiple_of(start + half * (self.rows // 2), 16), self.rows // 2)]
+
+    def own_copy(self):
+        k = self.k
+        return pltpu.make_async_copy(self.piece, self.spot(k.c, k.z, k.x, k.y), self.copy_sem)
+
+    def pass_on(self, z, source, when):
+        k = self.k
+        a, b = self.halves
+        whole = self.spot(k.c, z, k.x, k.y)
+        half = [self.spot(k.c, z, k.x, k.y, i) for i in range(2)]
+        if source is None:
+            parts = half
+            source = whole
+        else:
+            parts = [source.at[a], source.at[b]]
+        k.send(parts[0], half[0], self.at("g_xa", z), "x", when)
+        k.send(parts[1], half[1], self.at("g_yb", z), "y", when)
+        k.send(parts[0], half[0], self.at("g_ya", z), "y", when)
+        k.send(parts[1], half[1], self.at("g_xb", z), "x", when)
+        k.send(source, whole, self.at("g_c", z), "core", when)
+
+    def begin(self):
+        k = self.k
+        self.own_copy().start()
+        mine = self.spot(k.c, k.z, k.x, k.y)
+        k.send(self.piece, mine, self.at("g_up", k.z), "up", k.z < k.line - 1)
+        k.send(self.piece, mine, self.at("g_down", k.z), "down", k.z > 0)
+        self.pass_on(k.z, self.piece, None)
+
+    def along(self, r):
+        k = self.k
+        for sign, kind, way in ((-1, "g_up", "up"), (1, "g_down", "down")):
+            z = k.z + sign * r
+            here = (k.z >= r) if sign < 0 else (k.z + r < k.line)
+            place = self.spot(k.c, z, k.x, k.y)
+
+            @pl.when(here)
+            def _(place=place, kind=kind, z=z, way=way):
+                k.arrive(place, self.at(kind, z), way)
+
+            more = (k.z < k.line - 1) if sign < 0 else (k.z > 0)
+            k.send(place, place, self.at(kind, z), way, here & more)
+            self.pass_on(z, None, here)
+
+    def turn(self, z):
+        k = self.k
+        beside = self.spot(k.c, z, 1 - k.x, k.y, 0)
+        k.arrive(beside, self.at("g_xa", z), "x")
+        k.send(beside, beside, self.at("g_ya2", z), "y")
+        across = self.spot(k.c, z, k.x, 1 - k.y, 1)
+        k.arrive(across, self.at("g_yb", z), "y")
+        k.send(across, across, self.at("g_xb2", z), "x")
+
+    def share(self, z):
+        k = self.k
+        k.arrive(self.spot(k.c, z, k.x, 1 - k.y, 0), self.at("g_ya", z), "y")
+        across = self.spot(k.c, z, k.x, 1 - k.y)
+        k.send(across, across, self.at("g_c2", z), "core")
+        k.arrive(self.spot(k.c, z, 1 - k.x, k.y, 1), self.at("g_xb", z), "x")
+        k.arrive(self.spot(k.c, z, 1 - k.x, 1 - k.y, 0), self.at("g_ya2", z), "y")
+        k.arrive(self.spot(k.c, z, 1 - k.x, 1 - k.y, 1), self.at("g_xb2", z), "x")
+        for y in range(2):
+            beside = self.spot(k.c, z, 1 - k.x, y)
+            k.send(beside, beside, self.at("g_c3", z) if y == 0 else self.at("g_c3", z) + k.line, "core")
+
+    def end(self):
+        k = self.k
+        self.own_copy().wait()
+        other = 1 - k.c
+        for z in range(k.line):
+            k.arrive(self.spot(other, z, k.x, k.y), self.at("g_c", z), "core")
+            k.arrive(self.spot(other, z, k.x, 1 - k.y), self.at("g_c2", z), "core")
+            for y in range(2):
+                k.arrive(self.spot(other, z, 1 - k.x, y), self.at("g_c3", z) + y * k.line, "core")
+
+
+RS_SEMS = len(RS_KINDS)
+AG_SEMS = len(AG_KINDS) + 1
+
+
+def all_reduce_kernel(line, sizes, swaps, *refs):
+    count = len(sizes)
+    sources, near = refs[:count], refs[count : count + swaps]
+    out, far = refs[count + swaps], refs[count + swaps + 1 : count + 2 * swaps + 1]
+    scratch = refs[count + 2 * swaps + 1 :]
+    send_sems, recv_sems, load_sems, copy_sems = scratch[-4:]
+    links = Links(line, send_sems, recv_sems)
+    links.greet()
+    spare = count * (RS_SEMS + AG_SEMS) * line
+    scatters, gathers = [], []
+    top = 0
+    per_group = (RS_SEMS + AG_SEMS) * line
+    for g, size in enumerate(sizes):
+        rows = size // (8 * line)
+        buffers = scratch[8 * g : 8 * g + 8]
+        scatters.append(
+            Scatter(links, g * per_group, sources[g], 0, rows, *buffers, load_sems.at[g])
+        )
+
+        def index(c, z, x, y, top=top, rows=rows):
+            return top + (((c * line + z) * 2 + x) * 2 + y) * rows
+
+        gathers.append(
+            Gather(
+                links,
+                g * per_group + RS_SEMS * line,
+                buffers[0].at[links.z, links.x, links.y],
+                out,
+                rows,
+                index,
+                copy_sems.at[g],
+            )
+        )
+        top += size
+
+    def stage_first(g):
+        for z in scatters[g].order:
+            scatters[g].first(z)
+
+    def stage_second(g):
+        for z in scatters[g].order:
+            scatters[g].second(z)
+
+    def stage_third(g):
+        for z in scatters[g].order:
+            scatters[g].third(z)
+        scatters[g].last()
+        gathers[g].begin()
+
+    def stage_along(g):
+        for r in range(1, line):
+            gathers[g].along(r)
+
+    def stage_turn(g):
+        for z in range(line):
+            gathers[g].turn(z)
+
+    def stage_share(g):
+        for z in range(line):
+            gathers[g].share(z)
+
+    stages = [stage_first, stage_second, stage_third, stage_along, stage_turn, stage_share]
+    for g in range(count):
+        scatters[g].begin()
+    for i in range(swaps):
+        links.send(near[i], far[i], spare + i, "y")
+    for slot in range(len(stages) + count - 1):
+        for g in reversed(range(count)):
+            if 0 <= slot - g < len(stages):
+                stages[slot - g](g)
+    for g in range(count):
+        gathers[g].end()
+    for i in range(swaps):
+        links.arrive(far[i], spare + i, "y")
+    links.finish()
+
+
+def all_reduce(arrays, swaps, line, collective_id):
+    sizes = [a.shape[0] for a in arrays]
+    any_space = pl.BlockSpec(memory_space=pl.ANY)
+    scratch = []
+    for size in sizes:
+        rows = size // (8 * line)
+        half = rows // 2
+        scratch += [
+            pltpu.VMEM((line, 2, 2, rows, LANE), BF16),
+            pltpu.VMEM((line, 4 * rows, LANE), BF16),
+            pltpu.VMEM((line, 2, half, LANE), BF16),
+            pltpu.VMEM((line, 2, half, LANE), BF16),
+            pltpu.VMEM((line, half, LANE), BF16),
+            pltpu.VMEM((line, half, LANE), BF16),
+            pltpu.VMEM((line, rows, LANE), BF16),
+            pltpu.VMEM((line, rows, LANE), BF16),
+        ]
+    sems = len(sizes) * (RS_SEMS + AG_SEMS) * line + len(swaps)
+    scratch += [
+        pltpu.SemaphoreType.DMA((sems,)),
+        pltpu.SemaphoreType.DMA((sems,)),
+        pltpu.SemaphoreType.DMA((len(sizes), 4 * line)),
+        pltpu.SemaphoreType.DMA((len(sizes),)),
+    ]
+    return pl.pallas_call(
+        functools.partial(all_reduce_kernel, line, sizes, len(swaps)),
+        out_shape=[jax.ShapeDtypeStruct((sum(sizes), LANE), BF16)]
+        + [jax.ShapeDtypeStruct(s.shape, s.dtype) for s in swaps],
+        in_specs=[any_space] * (len(sizes) + len(swaps)),
+        out_specs=[any_space] * (1 + len(swaps)),
+        scratch_shapes=scratch,
+        compiler_params=pltpu.CompilerParams(
+            vmem_limit_bytes=56 * MIB, collective_id=collective_id, has_side_effects=True
+        ),
+        cost_estimate=pl.CostEstimate(flops=0, bytes_accessed=100 * MIB, transcendentals=0),
+        name="all_reduce",
+    )(*arrays, *swaps)
+
+
+def all_gather_kernel(line, swaps, piece, *refs):
+    near, out, far = refs[:swaps], refs[swaps], refs[swaps + 1 : 2 * swaps + 1]
+    send_sems, recv_sems, copy_sem = refs[2 * swaps + 1 :]
+    links = Links(line, send_sems, recv_sems)
+    links.greet()
+    spare = AG_SEMS * line
+    for i in range(swaps):
+        links.send(near[i], far[i], spare + i, "y")
+    rows = piece.shape[0] // 2
+
+    def index(c, z, x, y):
+        return (((z * 2 + x) * 2 + c) * 2 + y) * rows
+
+    mine = piece.at[pl.ds(pl.multiple_of(links.y * rows, 16), rows)]
+    gather = Gather(links, 0, mine, out, rows, index, copy_sem)
+    gather.begin()
+    for r in range(1, line):
+        gather.along(r)
+    for z in range(line):
+        gather.turn(z)
+    for z in range(line):
+        gather.share(z)
+    gather.end()
+    for i in range(swaps):
+        links.arrive(far[i], spare + i, "y")
+    links.finish()
+
+
+def all_gather(piece, swaps, line, collective_id):
+    any_space = pl.BlockSpec(memory_space=pl.ANY)
+    sems = AG_SEMS * line + len(swaps)
+    return pl.pallas_call(
+        functools.partial(all_gather_kernel, line, len(swaps)),
+        out_shape=[jax.ShapeDtypeStruct((4 * line * piece.shape[0], LANE), BF16)]
+        + [jax.ShapeDtypeStruct(s.shape, s.dtype) for s in swaps],
+        in_specs=[any_space] * (1 + len(swaps)),
+        out_specs=[any_space] * (1 + len(swaps)),
+        scratch_shapes=[
+            pltpu.SemaphoreType.DMA((sems,)),
+            pltpu.SemaphoreType.DMA((sems,)),
+            pltpu.SemaphoreType.DMA,
+        ],
+        compiler_params=pltpu.CompilerParams(collective_id=collective_id, has_side_effects=True),
+        cost_estimate=pl.CostEstimate(flops=0, bytes_accessed=100 * MIB, transcendentals=0),
+        name="all_gather",
+    )(piece, *swaps)
+
+
 def swap(value):
     return lax.ppermute(value, "seq", [(0, 1), (1, 0)])
 
@@ -628,9 +1073,13 @@
     tokens = tokens.reshape(half_len, D)
     firsts = first_values.reshape(half_len, HV)
     given = out_grad.reshape(half_len, D)
-    tokens_far, firsts_far = swap(tokens), swap(firsts)
+    line = dp_count // 4
     packed = pack_slots(masters)
-    slots = lax.all_gather(packed, "dp", axis=0, tiled=True)
+    if line == LINE:
+        slots, tokens_far, firsts_far = all_gather(packed, [tokens, firsts], line, 1)
+    else:
+        tokens_far, firsts_far = swap(tokens), swap(firsts)
+        slots = lax.all_gather(packed, "dp", axis=0, tiled=True)
 
     slot_index = slot_numbers(owners)
     slot_rows = owners * capacity + slot_index
@@ -665,14 +1114,16 @@
         tokens, att, given, w_out, w_up, w_down, vec
     )
     d_q, d_k, d_fresh, d_first = attend_back(q, k, v, att, grad_att, chance)
-    grad_near, grad_far, d_rest, vec_two = project_back(
-        tokens_all, n1, d_q, d_k, d_fresh, att, resid_low, w_qkv, vec
-    )
-    grad_back = swap(grad_far)
-    first_back = swap(d_first[half_len:].astype(BF16))
-    both = ("seq", "dp")
-    grads = lax.psum(jnp.concatenate([d_rest, d_up, d_down], axis=0), both)
-    vector_total = lax.psum((vec_one + vec_two).reshape(VEC), both)
+    grad_near, grad_far, d_rest = project_back(
+        tokens_all, n1, d_q, d_k, d_fresh, att, resid_low, w_qkv, vec, vec_one
+    )
+    first_far = d_first[half_len:].astype(BF16)
+    if line == LINE:
+        grads, grad_back, first_back = all_reduce([d_rest, d_up, d_down], [grad_far, first_far], line, 0)
+    else:
+        grad_back, first_back = swap(grad_far), swap(first_far)
+        grads = lax.psum(jnp.concatenate([d_rest, d_up, d_down], axis=0), ("seq", "dp"))
+    vector_total = grads[REST : REST + VEC // LANE].reshape(VEC).astype(F32)
 
     grad_n1 = grad_near + grad_back.astype(F32)
     hat, rate = normed(tokens.astype(F32))

time: 551 us -> 439 us (0.80)
  Pallas kernels: 125 us -> 408 us
  waiting for transfers between devices: 259 us -> 0 us
  blocking collectives: 78.1 us -> 0 us
  other arithmetic: 51.3 us -> 8.1 us
  between operations: 14.3 us -> 0.98 us
    pallas_call x0 -> x2, Pallas kernels: none -> 285 us  [the longest x1 166 us: all_reduce(): pl.pallas_call(functools.partial(all_reduce_kernel, line, sizes, len(swap...]
    psum x1 -> x0, waiting for transfers between devices: 154 us -> none  [shards(): grads = lax.psum(jnp.concatenate([d_rest, d_up, d_down], axis=0), both)]
    all_gather x1 -> x0, waiting for transfers between devices: 80.2 us -> none  [shards(): slots = lax.all_gather(packed, 'dp', axis=0, tiled=True)]
    psum x1 -> x0, blocking collectives: 78.1 us -> none  [shards(): vector_total = lax.psum((vec_one + vec_two).reshape(VEC), both)]
    concatenate x1 -> x0, other arithmetic: 38.2 us -> none  [shards(): grads = lax.psum(jnp.concatenate([d_rest, d_up, d_down], axis=0), both)]
    ppermute x4 -> x0, waiting for transfers between devices: 25.2 us -> none  [swap(): return lax.ppermute(value, 'seq', [(0, 1), (1, 0)])]
    unnamed x60 -> x64, local copies, waits for them, and re-layouts: 14.9 us -> 15.5 us
  transfers between devices with their start and end apart: 6 -> 0, of which waited for: 3 -> 0; matrix products, arithmetic and copies ran while one was open for 3% -> 0% of each run, Pallas kernels for 0% -> 0%
where the time goes in v3:
time: 439 us; the launch traced here: 435 us
  Pallas kernels  408 us (93%)
  local copies, waits for them, and re-layouts  18.5 us (4%)
  other arithmetic  8.1 us (2%)
    pallas_call x1, Pallas kernels, all_reduce(): pl.pallas_call(functools.partial(all_reduce_kernel, line, sizes, len(swap...  166 us
    pallas_call x1, Pallas kernels, all_gather(): pl.pallas_call(functools.partial(all_gather_kernel, line, len(swaps)), ou...  119 us
    pallas_call x1, Pallas kernels, hidden(): pl.pallas_call(hidden_kernel, out_shape=[jax.ShapeDtypeStruct(line, BF16)...  31.5 us
    pallas_call x1, Pallas kernels, attend(): pl.pallas_call(attend_kernel, out_shape=[jax.ShapeDtypeStruct((queries, D...  25.2 us
    pallas_call x1, Pallas kernels, attend_back(): pl.pallas_call(attend_back_kernel, out_shape=[jax.ShapeDtypeStruct((queri...  24.6 us
    unnamed x64, local copies, waits for them, and re-layouts  15.5 us
    pallas_call x1, Pallas kernels, project_back(): pl.pallas_call(project_back_kernel, out_shape=[jax.ShapeDtypeStruct((rows...  12.9 us
    pallas_call x1, Pallas kernels, unpack_weights(): pl.pallas_call(unpack_kernel, out_shape=[jax.ShapeDtypeStruct(s, BF16) fo...  10.3 us

profile of v3, /device:TPU:0, one launch (start us, length us, event | category | flops | bytes accessed | tf_op | source)
XLA Modules:
  0.0 435.4 jit_solution(7731275761092737605)
XLA Ops:
  0.7 0.8 pad_add_fusion
  1.9 1.7 copy-done
  3.6 1.7 pack_slots.1.piece
  5.3 1.0 copy-done.2
  6.4 118.7 %all_gather.1 = (bf16[81920,128]{1,0:T(8,128)(2,1)}, bf16[512,768]{1,0:T(8,128)(2,1)}, bf16[512,384]{1,0:T(8,128)(2,1)}) custom-call(bf16[5120,128]{1,0:T(8,128)(2,1)} %copy-done.2, bf16[512,768]{1,0:T(8,128)(2,1)} %bitcast.30, bf16[512,384]{1,0:T(8,128)(2,1)} %bitcast.33), custom_call_target="tpu_custom_call" | custom-call | bytes 104857600 | tf_op jit(solution)/shard_map/all_gather/pallas_call | solution.py:1032
  125.4 10.3 %unpack_weights.1 = (bf16[768,1920]{1,0:T(8,128)(2,1)S(1)}, bf16[768,768]{1,0:T(8,128)(2,1)S(1)}, bf16[768,3072]{1,0:T(8,128)(2,1)}, bf16[3072,768]{1,0:T(8,128)(2,1)}) custom-call(s32[414]{0:T(512)S(1)} %multiply_add_fusion.1.slot_rows, bf16[81920,128]{1,0:T(8,128)(2,1)} %get-tuple-element.46.slots), custom_call_target="tpu_custom_call" | custom-call | bytes 27131904 | tf_op jit(solution)/shard_map/unpack_weights/pallas_call | solution.py:185
  135.7 1.0 copy-done.12
  136.7 1.2 pad_maximum_fusion.tokens
  137.9 0.8 copy-done.10
  138.9 0.7 copy-done.26
  139.6 7.9 %project.1 = (bf16[1024,768]{1,0:T(8,128)(2,1)S(1)}, bf16[512,768]{1,0:T(8,128)(2,1)S(1)}, bf16[1024,768]{1,0:T(8,128)(2,1)S(1)}, bf16[1024,768]{1,0:T(8,128)(2,1)}) custom-call(bf16[1024,768]{1,0:T(8,128)(2,1)} %pad_maximum_fusion.tokens, bf16[1024,384]{1,0:T(8,128)(2,1)S(1)} %pad_maximum_fusion.1.firsts, bf16[768,1920]{1,0:T(8,128)(2,1)} %copy-done.10, ...), custom_call_target="tpu_custom_call" | custom-call | flops 3019898880 | bytes 10813440 | tf_op jit(solution)/shard_map/project/pallas_call | solution.py:226
  147.5 2.5 copy-done.5
  150.1 25.2 %attend.1 = (bf16[512,768]{1,0:T(8,128)(2,1)S(1)}, bf16[12,1024,512]{2,1,0:T(8,128)(2,1)}) custom-call(bf16[512,768]{1,0:T(8,128)(2,1)S(1)} %get-tuple-element.48.q, bf16[1024,768]{1,0:T(8,128)(2,1)S(1)} %get-tuple-element.49.k, bf16[1024,768]{1,0:T(8,128)(2,1)S(1)} %copy-done.5, s32[1,512]{1,0:T(1,128)S(1)} %bitcast.29, s32[1024,1]{1,0:T(8,128)S(1)} %bitcast.28), custom_call_target="tpu_custom_call" | custom-call | flops 1610612736 | bytes 12582912 | tf_op jit(solution)/shard_map/attend/pallas_call | solution.py:281
  175.2 0.9 copy-done.6
  176.1 31.5 %hidden.1 = (bf16[512,768]{1,0:T(8,128)(2,1)}, f32[512,768]{1,0:T(8,128)}, bf16[512,768]{1,0:T(8,128)(2,1)}, bf16[512,768]{1,0:T(8,128)(2,1)}, bf16[18432,128]{1...) custom-call(bf16[512,768]{1,0:T(8,128)(2,1)} %bitcast.31, bf16[512,768]{1,0:T(8,128)(2,1)} %copy-done.6, ...), custom_call_target="tpu_custom_call" | custom-call | flops 15703474176 | bytes 26738688 | tf_op jit(solution)/shard_map/hidden/pallas_call | solution.py:380
  207.6 1.1 copy-done.8
  208.7 24.6 %attend_back.1 = (bf16[512,768]{1,0:T(8,128)(2,1)S(1)}, bf16[1024,768]{1,0:T(8,128)(2,1)S(1)}, bf16[1024,384]{1,0:T(8,128)(2,1)S(1)}, f32[1024,384]{1,0:T(8,128)}) custom-call(bf16[512,768]{1,0:T(8,128)(2,1)S(1)} %get-tuple-element.48.q, bf16[1024,768]{1,0:T(8,128)(2,1)} %copy-done.4, bf16[1024,768]{1,0:T(8,128)(2,1)} %get-tuple-element.50.v, ...), custom_call_target="tpu_custom_call" | custom-call | flops 3221225472 | bytes 12582912 | tf_op jit(solution)/shard_map/attend_back/pallas_call | solution.py:454
  233.3 1.1 copy-done.11
  234.4 0.9 copy-done.13
  235.3 0.9 copy-done.14
  236.2 12.9 %project_back.1 = (f32[512,768]{1,0:T(8,128)}, bf16[512,768]{1,0:T(8,128)(2,1)}, bf16[16384,128]{1,0:T(8,128)(2,1)}) custom-call(bf16[1024,768]{1,0:T(8,128)(2,1)} %pad_maximum_fusion.tokens, bf16[1024,768]{1,0:T(8,128)(2,1)} %copy-done.15, bf16[512,768]{1,0:T(8,128)(2,1)} %copy-done.13, bf16[1024,768]{1,0:T(8,128)(2,1)} %copy-done.11, ...), custom_call_target="tpu_custom_call" | custom-call | flops 4227858432 | bytes 14680064 | tf_op jit(solution)/shard_map/project_back/pallas_call | solution.py:525
  249.1 1.9 slice.31.refs_4_
  251.0 166.4 %all_reduce.1 = (bf16[53248,128]{1,0:T(8,128)(2,1)}, bf16[512,768]{1,0:T(8,128)(2,1)}, bf16[512,384]{1,0:T(8,128)(2,1)}) custom-call(bf16[16384,128]{1,0:T(8,128)(2,1)} %get-tuple-element.66.refs_0_, bf16[18432,128]{1,0:T(8,128)(2,1)} %get-tuple-element.67.refs_1_, bf16[18432,128]{1,0:T(8,128)(2,1)} %get-tuple-element.68.refs_2_, ...), custom_call_target="tpu_custom_call" | custom-call | bytes 104857600 | tf_op jit(solution)/shard_map/all_reduce/pallas_call | solution.py:986
  417.8 1.7 copy-done.3
  419.6 8.8 %adam.1 = (f32[40,16384]{1,0:T(8,128)}, f32[40,16384]{1,0:T(8,128)}, f32[40,16384]{1,0:T(8,128)}, bf16[40,16384]{1,0:T(8,128)(2,1)}) custom-call(s32[40]{0:T(128)S(1)} %fusion.16.places, bf16[53248,128]{1,0:T(8,128)(2,1)} %get-tuple-element.73.grads, f32[40,128]{1,0:T(8,128)S(1)} %broadcast_in_dim.26.used, f32[40,16384]{1,0:T(8,128)S(1)} %copy-done.1, ...), custom_call_target="tpu_custom_call" | custom-call | flops 13107200 | bytes 18350080 | tf_op jit(solution)/shard_map/adam/pallas_call | solution.py:580
  428.4 0.9 add_bitcast_fusion
  429.4 0.9 slice_reduce_fusion
  430.5 0.4 fusion.9
  430.9 0.7 fusion.11
  431.6 0.7 copy-done.21
  432.3 1.8 fusion.8
  434.1 1.4 multiply_subtract_fusion
  (67 shorter events, 1.4 us)
Async XLA Ops:
  1.9 1.7 copy-start
  5.3 1.1 copy-start.2
  6.4 118.7 %copy-start.29 = (s32[414]{0:T(512)S(1)}, s32[414]{0:T(512)}, u32[]{:S(2)}) copy-start(s32[414]{0:T(512)} %param.15) | copy-start | bytes 4972
  125.3 11.3 %copy-start.16 = (bf16[1,512,768]{2,1,0:T(8,128)(2,1)S(1)}, bf16[1,512,768]{2,1,0:T(8,128)(2,1)}, u32[]{:S(2)}) copy-start(bf16[1,512,768]{2,1,0:T(8,128)(2,1)} %param.11) | copy-start | bytes 2359300
  125.3 11.3 %copy-start.23 = (bf16[512,768]{1,0:T(8,128)(2,1)S(1)}, bf16[512,768]{1,0:T(8,128)(2,1)}, u32[]{:S(2)}) copy-start(bf16[512,768]{1,0:T(8,128)(2,1)} %get-tuple-element.44) | copy-start | bytes 2359300
  135.6 1.0 copy-start.12
  136.7 2.1 copy-start.10
  136.7 2.1 copy-start.20
  136.7 2.1 copy-start.24
  138.8 0.8 copy-start.26
  139.6 7.9 %copy-start.9 = (f32[1,8832]{1,0:T(1,128)}, f32[1,8832]{1,0:T(1,128)S(1)}, u32[]{:S(2)}) copy-start(f32[1,8832]{1,0:T(1,128)S(1)} %reshape.106.vec) | copy-start | bytes 105988
  147.5 27.7 %copy-start.4 = (bf16[1024,768]{1,0:T(8,128)(2,1)}, bf16[1024,768]{1,0:T(8,128)(2,1)S(1)}, u32[]{:S(2)}) copy-start(bf16[1024,768]{1,0:T(8,128)(2,1)S(1)} %get-tuple-element.49.k) | copy-start | bytes 4718596
  147.5 27.7 %copy-start.15 = (bf16[1024,768]{1,0:T(8,128)(2,1)}, bf16[1024,768]{1,0:T(8,128)(2,1)S(1)}, u32[]{:S(2)}) copy-start(bf16[1024,768]{1,0:T(8,128)(2,1)S(1)} %get-tuple-element.57.n1) | copy-start | bytes 4718596
  147.5 2.5 copy-start.5
  175.2 0.9 copy-start.6
  176.1 31.5 %copy-start.7 = (bf16[512,768]{1,0:T(8,128)(2,1)S(1)}, bf16[512,768]{1,0:T(8,128)(2,1)}, u32[]{:S(2)}) copy-start(bf16[512,768]{1,0:T(8,128)(2,1)} %copy-done.6) | copy-start | bytes 2359300
  207.6 1.1 copy-start.8
  233.3 1.1 copy-start.11
  234.4 0.9 copy-start.13
  235.3 0.9 copy-start.14
  251.0 166.8 %copy-start.1 = (f32[40,16384]{1,0:T(8,128)S(1)}, f32[40,16384]{1,0:T(8,128)}, u32[]{:S(2)}) copy-start(f32[40,16384]{1,0:T(8,128)} %weight.1) | copy-start | bytes 7864324
  417.8 1.7 copy-start.3
  419.6 8.8 %copy-start.22 = (f32[1024,384]{1,0:T(8,128)S(1)}, f32[1024,384]{1,0:T(8,128)}, u32[]{:S(2)}) copy-start(f32[1024,384]{1,0:T(8,128)} %get-tuple-element.70) | copy-start | bytes 4718596
  419.6 8.8 %copy-start.25 = (bf16[512,384]{1,0:T(8,128)(2,1)S(1)}, bf16[512,384]{1,0:T(8,128)(2,1)}, u32[]{:S(2)}) copy-start(bf16[512,384]{1,0:T(8,128)(2,1)} %get-tuple-element.72) | copy-start | bytes 1179652
  428.4 1.9 copy-start.17
  428.4 2.5 copy-start.18
  428.4 2.5 copy-start.19
  430.9 1.4 copy-start.21
  432.3 1.8 copy-start.27
  432.3 1.8 copy-start.28

commit v4 on v2

--- a/solution.py
+++ b/solution.py
@@ -17,6 +17,8 @@
 FF_STEP = 512
 VEC = 7 * D + HV + FF
 MIB = 1024 * 1024
+LINE = 4
+REST = 126 * LANE
 
 EPS_NORM = 1e-05
 EPS_ADAM = 1e-08
@@ -479,7 +481,7 @@
 
 
 def project_back_kernel(
-    tokens, n1, d_q, d_k, d_fresh, att, resid_low, w_qkv, vec,
+    tokens, n1, d_q, d_k, d_fresh, att, resid_low, w_qkv, vec, vec_one,
     grad_near, grad_far, d_rest, vec_grad, flat,
 ):
     rows = n1.shape[0] // 2
@@ -490,7 +492,7 @@
     grad_near[...] = near
     grad_far[...] = far.astype(BF16)
     hat, _ = normed(tokens[...].astype(F32))
-    vec_grad[...] = jnp.zeros_like(vec_grad)
+    vec_grad[...] = vec_one[...]
     vec_grad[:, :D] = jnp.sum(near * hat[:rows], axis=0, keepdims=True) + jnp.sum(
         far * hat[rows:], axis=0, keepdims=True
     )
@@ -511,11 +513,13 @@
         for j in range(columns):
             flat[pl.ds(j, D, stride=columns), :] = product[:, j * LANE : (j + 1) * LANE]
         d_rest[start : start + size] = flat[:size].astype(BF16)
-    used = 3 * D * per_row + D * HV // LANE
-    d_rest[used:] = jnp.zeros((d_rest.shape[0] - used, LANE), BF16)
-
-
-def project_back(tokens, n1, d_q, d_k, d_fresh, att, resid_low, w_qkv, vec):
+    flat[: 2 * LANE] = jnp.zeros((2 * LANE, LANE), F32)
+    for j in range(VEC // LANE):
+        flat[j : j + 1] = vec_grad[:, j * LANE : (j + 1) * LANE]
+    d_rest[REST:] = flat[: 2 * LANE].astype(BF16)
+
+
+def project_back(tokens, n1, d_q, d_k, d_fresh, att, resid_low, w_qkv, vec, vec_one):
     rows = n1.shape[0] // 2
     vm = pl.BlockSpec(memory_space=pltpu.VMEM)
     return pl.pallas_call(
@@ -524,15 +528,14 @@
             jax.ShapeDtypeStruct((rows, D), F32),
             jax.ShapeDtypeStruct((rows, D), BF16),
             jax.ShapeDtypeStruct((128 * LANE, LANE), BF16),
-            jax.ShapeDtypeStruct((1, VEC), F32),
-        ],
-        in_specs=[vm] * 9,
-        out_specs=[vm] * 4,
-        scratch_shapes=[pltpu.VMEM((D * D // LANE, LANE), F32)],
+        ],
+        in_specs=[vm] * 10,
+        out_specs=[vm] * 3,
+        scratch_shapes=[pltpu.VMEM((1, VEC), F32), pltpu.VMEM((D * D // LANE, LANE), F32)],
         compiler_params=params(58),
         cost_estimate=cost(2 * rows * D * (7 * D), 14 * MIB),
         name="project_back",
-    )(tokens, n1, d_q, d_k, d_fresh, att, resid_low, w_qkv, vec)
+    )(tokens, n1, d_q, d_k, d_fresh, att, resid_low, w_qkv, vec, vec_one)
 
 
 def adam_kernel(places, grads, used, weight, one, two, new, new_one, new_two, low, stage, flat, sems):
@@ -601,6 +604,803 @@
     )(places, grads, used, weight, one, two)
 
 
+class Links:
+    def __init__(self, line, send_sems, recv_sems):
+        dp = lax.axis_index("dp")
+        self.line = line
+        self.y = lax.axis_index("seq")
+        self.z = dp // 4
+        self.x = (dp // 2) % 2
+        self.c = dp % 2
+        self.send_sems, self.recv_sems = send_sems, recv_sems
+        self.to = {
+            "core": {"dp": self.z * 4 + self.x * 2 + (1 - self.c)},
+            "x": {"dp": self.z * 4 + (1 - self.x) * 2 + self.c},
+            "y": {"seq": 1 - self.y},
+            "up": {"dp": dp + 4},
+            "down": {"dp": dp - 4},
+        }
+        self.sent = []
+
+    def greet(self, whole_line):
+        barrier = pltpu.get_barrier_semaphore()
+        for name in ("core", "x", "y"):
+            pl.semaphore_signal(barrier, inc=1, device_id=self.to[name])
+        if whole_line:
+            for d in range(1, self.line):
+                z = (self.z + d) % self.line
+                pl.semaphore_signal(barrier, inc=1, device_id={"dp": z * 4 + self.x * 2 + self.c})
+            pl.semaphore_wait(barrier, 2 + self.line)
+            return
+
+        @pl.when(self.z > 0)
+        def _():
+            pl.semaphore_signal(barrier, inc=1, device_id=self.to["down"])
+
+        @pl.when(self.z < self.line - 1)
+        def _():
+            pl.semaphore_signal(barrier, inc=1, device_id=self.to["up"])
+
+        pl.semaphore_wait(
+            barrier,
+            3 + jnp.where(self.z > 0, 1, 0) + jnp.where(self.z < self.line - 1, 1, 0),
+        )
+
+    def copy(self, source, target, index, way):
+        sender, receiver = index if isinstance(index, tuple) else (index, index)
+        to = self.to[way] if isinstance(way, str) else {"dp": way * 4 + self.x * 2 + self.c}
+        return pltpu.make_async_remote_copy(
+            src_ref=source,
+            dst_ref=target,
+            send_sem=self.send_sems.at[sender],
+            recv_sem=self.recv_sems.at[receiver],
+            device_id=to,
+        )
+
+    def send(self, describe):
+        source, target, index, way, when = describe()
+        if when is None:
+            self.copy(source, target, index, way).start()
+        else:
+
+            @pl.when(when)
+            def _():
+                self.copy(source, target, index, way).start()
+
+        self.sent.append(describe)
+
+    def arrive(self, target, index, way):
+        self.copy(target, target, index, way).wait_recv()
+
+    def finish(self):
+        for describe in self.sent:
+            source, target, index, way, when = describe()
+            if when is None:
+                self.copy(source, target, index, way).wait_send()
+            else:
+
+                @pl.when(when)
+                def _(source=source, target=target, index=index, way=way):
+                    self.copy(source, target, index, way).wait_send()
+
+
+def add_into(place, *others):
+    total = place[...].astype(F32)
+    for other in others:
+        total = total + other[...].astype(F32)
+    place[...] = total.astype(BF16)
+
+
+class Scatter:
+    KINDS = ("core", "xa", "yb", "ya", "xb", "to", "from")
+
+    def __init__(self, links, base, source, offset, rows, cut, buffers, load_sems):
+        self.k, self.base, self.source, self.offset, self.rows = links, base, source, offset, rows
+        self.held, self.r_core, self.r_xa, self.r_yb, self.r_ya, self.r_xb, self.r_line = buffers
+        self.load_sems = load_sems
+        self.halves = (pl.ds(0, cut), pl.ds(cut, rows - cut))
+
+    @staticmethod
+    def buffers_of(rows, cut, line):
+        return [
+            pltpu.VMEM((line, 2, 2, rows, LANE), BF16),
+            pltpu.VMEM((line, 4 * rows, LANE), BF16),
+            pltpu.VMEM((line, 2, cut, LANE), BF16),
+            pltpu.VMEM((line, 2, rows - cut, LANE), BF16),
+            pltpu.VMEM((line, cut, LANE), BF16),
+            pltpu.VMEM((line, rows - cut, LANE), BF16),
+            pltpu.VMEM((line, rows, LANE), BF16),
+        ]
+
+    def at(self, kind, z):
+        return self.base + self.KINDS.index(kind) * self.k.line + z
+
+    def load(self, z):
+        start = self.offset + (self.k.c * self.k.line + z) * 4 * self.rows
+        return [
+            pltpu.make_async_copy(
+                self.source.at[pl.ds(pl.multiple_of(start + i * self.rows, 16), self.rows)],
+                self.held.at[z, i // 2, i % 2],
+                self.load_sems.at[4 * z + i],
+            )
+            for i in range(4)
+        ]
+
+    def begin(self):
+        k = self.k
+
+        def describe(z):
+            start = self.offset + ((1 - k.c) * k.line + z) * 4 * self.rows
+            source = self.source.at[pl.ds(pl.multiple_of(start, 16), 4 * self.rows)]
+            return source, self.r_core.at[z], self.at("core", z), "core", None
+
+        for z in range(k.line):
+            k.send(functools.partial(describe, z))
+            for copy in self.load(z):
+                copy.start()
+
+    def first(self, z):
+        k, (a, b) = self.k, self.halves
+        for copy in self.load(z):
+            copy.wait()
+        k.arrive(self.r_core.at[z], self.at("core", z), "core")
+        for i in range(4):
+            add_into(self.held.at[z, i // 2, i % 2], self.r_core.at[z, pl.ds(i * self.rows, self.rows)])
+        k.send(lambda: (self.held.at[z, 1 - k.x, :, a], self.r_xa.at[z], self.at("xa", z), "x", None))
+        k.send(lambda: (self.held.at[z, :, 1 - k.y, b], self.r_yb.at[z], self.at("yb", z), "y", None))
+
+    def second(self, z):
+        k, (a, b) = self.k, self.halves
+        k.arrive(self.r_xa.at[z], self.at("xa", z), "x")
+        for y in range(2):
+            add_into(self.held.at[z, k.x, y, a], self.r_xa.at[z, y])
+        k.send(lambda: (self.held.at[z, k.x, 1 - k.y, a], self.r_ya.at[z], self.at("ya", z), "y", None))
+        k.arrive(self.r_yb.at[z], self.at("yb", z), "y")
+        for x in range(2):
+            add_into(self.held.at[z, x, k.y, b], self.r_yb.at[z, x])
+        k.send(lambda: (self.held.at[z, 1 - k.x, k.y, b], self.r_xb.at[z], self.at("xb", z), "x", None))
+
+    def third(self, z):
+        k, (a, b) = self.k, self.halves
+        k.arrive(self.r_ya.at[z], self.at("ya", z), "y")
+        add_into(self.held.at[z, k.x, k.y, a], self.r_ya.at[z])
+        k.arrive(self.r_xb.at[z], self.at("xb", z), "x")
+        add_into(self.held.at[z, k.x, k.y, b], self.r_xb.at[z])
+
+        def describe():
+            index = (self.at("to", z), self.at("from", k.z))
+            return self.held.at[z, k.x, k.y], self.r_line.at[k.z], index, z, k.z != z
+
+        k.send(describe)
+
+    def last(self):
+        k = self.k
+        others = [(k.z + d) % k.line for d in range(1, k.line)]
+        for z in others:
+            k.arrive(self.r_line.at[z], (self.at("to", z), self.at("from", z)), z)
+        add_into(self.held.at[k.z, k.x, k.y], *[self.r_line.at[z] for z in others])
+
+
+class Spread:
+    KINDS = ("to", "from", "xa", "yb", "ya", "xb", "ya2", "xb2", "c0", "c1", "c2", "c3")
+
+    def __init__(self, links, base, own, out, index, rows, cut):
+        self.k, self.base, self.own, self.out, self.index = links, base, own, out, index
+        self.parts = {None: (0, rows), 0: (0, cut), 1: (cut, rows - cut)}
+
+    def at(self, kind, z):
+        return self.base + self.KINDS.index(kind) * self.k.line + z
+
+    def spot(self, z, other_x, other_y, half=None, core=None):
+        k = self.k
+        c = k.c if core is None else core
+        x = 1 - k.x if other_x else k.x
+        y = 1 - k.y if other_y else k.y
+        first, count = self.parts[half]
+        return self.out.at[pl.ds(pl.multiple_of(self.index(c, z, x, y) + first, 16), count)]
+
+    def place(self, d):
+        return (self.k.z + d) % self.k.line
+
+    def give(self, kind, way, d, other_x=False, other_y=False, half=None, own=False):
+        def describe():
+            z = self.place(d)
+            target = self.spot(z, other_x, other_y, half)
+            source = self.own(half) if own else target
+            return source, target, self.at(kind, z), way, None
+
+        self.k.send(describe)
+
+    def get(self, kind, way, d, other_x=False, other_y=False, half=None):
+        z = self.place(d)
+        self.k.arrive(self.spot(z, other_x, other_y, half), self.at(kind, z), way)
+
+    def cross(self, d):
+        own = d == 0
+        self.give("xa", "x", d, half=0, own=own)
+        self.give("yb", "y", d, half=1, own=own)
+        self.give("ya", "y", d, half=0, own=own)
+        self.give("xb", "x", d, half=1, own=own)
+        self.give("c0", "core", d, own=own)
+
+    def start(self):
+        k = self.k
+
+        def describe(d):
+            z = self.place(d)
+            return self.own(None), self.spot(k.z, False, False), (self.at("to", z), self.at("from", k.z)), z, None
+
+        for d in (k.line - 1, 1, 2):
+            k.send(functools.partial(describe, d))
+        self.cross(0)
+
+    def along(self, d):
+        z = self.place(d)
+        self.k.arrive(self.spot(z, False, False), (self.at("to", z), self.at("from", z)), z)
+        self.cross(d)
+
+    def turn(self, d):
+        self.get("xa", "x", d, other_x=True, half=0)
+        self.give("ya2", "y", d, other_x=True, half=0)
+        self.get("yb", "y", d, other_y=True, half=1)
+        self.give("xb2", "x", d, other_y=True, half=1)
+
+    def share(self, d):
+        self.get("ya", "y", d, other_y=True, half=0)
+        self.give("c1", "core", d, other_y=True)
+        self.get("xb", "x", d, other_x=True, half=1)
+        self.give("c2", "core", d, other_x=True)
+        self.get("ya2", "y", d, other_x=True, other_y=True, half=0)
+        self.get("xb2", "x", d, other_x=True, other_y=True, half=1)
+        self.give("c3", "core", d, other_x=True, other_y=True)
+
+    def end(self):
+        k = self.k
+        for z in range(k.line):
+            for i in range(4):
+                k.arrive(self.spot(z, i >= 2, i % 2 == 1, core=1 - k.c), self.at(f"c{i}", z), "core")
+
+
+RS_SEMS = len(Scatter.KINDS)
+AR_SEMS = RS_SEMS + len(Spread.KINDS)
+
+
+class Total:
+    def __init__(self, links, base, source, offset, kind, out, top, buffers, load_sems, copy_sem):
+        line = links.line
+        size, cut, turn = kind
+        rows = size // (8 * line)
+        held = buffers[0]
+
+        def index(c, z, x, y):
+            return top + (((c * line + z) * 2 + x) * 2 + y) * rows
+
+        def own(half):
+            first, count = {None: (0, rows), 0: (0, turn), 1: (turn, rows - turn)}[half]
+            return held.at[links.z, links.x, links.y, pl.ds(first, count)]
+
+        self.line = line
+        self.scatter = Scatter(links, base, source, offset, rows, cut, buffers, load_sems)
+        self.spread = Spread(links, base + RS_SEMS * line, own, out, index, rows, turn)
+        self.copy_sem = copy_sem
+
+    def keep(self):
+        g = self.spread
+        return pltpu.make_async_copy(g.own(None), g.spot(g.k.z, False, False), self.copy_sem)
+
+    def run(self, stage, part):
+        scatter, spread = self.scatter, self.spread
+        if stage == 0:
+            scatter.begin()
+        elif stage < 4:
+            (scatter.first, scatter.second, scatter.third)[stage - 1](part)
+        elif stage == 4:
+            scatter.last()
+            self.keep().start()
+            spread.start()
+        elif stage == 5:
+            spread.along(part + 1)
+        elif stage < 8:
+            (spread.turn, spread.share)[stage - 6](part)
+        else:
+            self.keep().wait()
+            spread.end()
+
+    def parts(self, stage):
+        return (1, 4, 4, 4, 1, 3, 4, 4, 1)[stage]
+
+
+class Gather:
+    KINDS = ("up", "down", "xa", "yb", "ya", "xb", "ya2", "xb2", "x2") + tuple(
+        f"{way}{i}" for way in ("u", "d", "c") for i in range(4)
+    )
+
+    def __init__(self, links, base, own, out, index, first, rows, cut, z_first, twice):
+        self.k, self.base, self.own, self.out, self.index = links, base, own, out, index
+        self.parts = {None: (first, rows), 0: (first, cut), 1: (first + cut, rows - cut)}
+        self.z_first, self.twice = z_first, twice
+
+    def at(self, kind, z):
+        return self.base + self.KINDS.index(kind) * self.k.line + z
+
+    def spot(self, z, other_x, other_y, half=None, core=None):
+        k = self.k
+        c = k.c if core is None else core
+        x = 1 - k.x if other_x else k.x
+        y = 1 - k.y if other_y else k.y
+        first, count = self.parts[half]
+        return self.out.at[pl.ds(pl.multiple_of(self.index(c, z, x, y) + first, 16), count)]
+
+    def give(self, kind, way, z, other_x=False, other_y=False, half=None, when=None, own=False):
+        def describe():
+            place = self.spot(z(), other_x, other_y, half)
+            source = self.own(other_y, half) if own else place
+            return source, place, self.at(kind, z()), way, None if when is None else when()
+
+        self.k.send(describe)
+
+    def get(self, kind, way, z, other_x=False, other_y=False, half=None):
+        self.k.arrive(self.spot(z, other_x, other_y, half), self.at(kind, z), way)
+
+    def near(self):
+        k = self.k
+        found = []
+        for r in range(1, k.line):
+            found.append(
+                (
+                    lambda r=r: k.z - r,
+                    lambda r=r: k.z >= r,
+                    "u",
+                    "up",
+                    lambda r=r: (k.z >= r) & (k.z < k.line - 1),
+                )
+            )
+            found.append(
+                (
+                    lambda r=r: k.z + r,
+                    lambda r=r: k.z + r < k.line,
+                    "d",
+                    "down",
+                    lambda r=r: (k.z + r < k.line) & (k.z > 0),
+                )
+            )
+        return found
+
+    def here(self):
+        return self.k.z
+
+    def lower(self):
+        return self.k.z < self.k.line - 1
+
+    def upper(self):
+        return self.k.z > 0
+
+    def cross(self, z, when, own):
+        self.give("xa", "x", z, half=0, when=when, own=own)
+        self.give("yb", "y", z, half=1, when=when, own=own)
+        self.give("ya", "y", z, half=0, when=when, own=own)
+        self.give("xb", "x", z, half=1, when=when, own=own)
+        self.give("c0", "core", z, when=when, own=own)
+
+    def start(self):
+        self.give("up", "up", self.here, when=self.lower, own=True)
+        self.give("down", "down", self.here, when=self.upper, own=True)
+        if self.twice:
+            for other, kind in ((False, "xa"), (True, "x2")):
+                self.give(kind, "x", self.here, other_y=other, own=True)
+                self.give("c1" if other else "c0", "core", self.here, other_y=other, own=True)
+        else:
+            self.cross(self.here, None, True)
+
+    def along(self, number):
+        z, exists, _, way, goes_on = self.near()[number]
+
+        @pl.when(exists())
+        def _():
+            self.get(way, way, z())
+
+        self.give(way, way, z, when=goes_on)
+        self.cross(z, exists, False)
+
+    def turn(self, z, when):
+        def waits():
+            self.get("xa", "x", z(), other_x=True, half=0)
+
+        def waits_too():
+            self.get("yb", "y", z(), other_y=True, half=1)
+
+        waits() if when is None else pl.when(when())(waits)
+        self.give("ya2", "y", z, other_x=True, half=0, when=when)
+        waits_too() if when is None else pl.when(when())(waits_too)
+        self.give("xb2", "x", z, other_y=True, half=1, when=when)
+
+    def share(self, z, when):
+        def waits(kind, way, **place):
+            def wait():
+                self.get(kind, way, z(), **place)
+
+            wait() if when is None else pl.when(when())(wait)
+
+        waits("ya", "y", other_y=True, half=0)
+        self.give("c1", "core", z, other_y=True, when=when)
+        waits("xb", "x", other_x=True, half=1)
+        self.give("c2", "core", z, other_x=True, when=when)
+        waits("ya2", "y", other_x=True, other_y=True, half=0)
+        waits("xb2", "x", other_x=True, other_y=True, half=1)
+        self.give("c3", "core", z, other_x=True, other_y=True, when=when)
+
+    def share_twice(self):
+        for other, kind in ((False, "xa"), (True, "x2")):
+            self.get(kind, "x", self.k.z, other_x=True, other_y=other)
+            self.give("c3" if other else "c2", "core", self.here, other_x=True, other_y=other)
+
+    def lift(self, i, own=False):
+        place = dict(other_x=i >= 2, other_y=i % 2 == 1)
+        self.give(f"u{i}", "up", self.here, when=self.lower, own=own, **place)
+        self.give(f"d{i}", "down", self.here, when=self.upper, own=own, **place)
+        self.give(f"c{i}", "core", self.here, own=own, **place)
+
+    def start_plane(self):
+        if self.twice:
+            for other, kind in ((False, "xa"), (True, "x2")):
+                self.give(kind, "x", self.here, other_y=other, own=True)
+            self.lift(0, True)
+            self.lift(1, True)
+        else:
+            self.give("xa", "x", self.here, half=0, own=True)
+            self.give("yb", "y", self.here, half=1, own=True)
+            self.give("ya", "y", self.here, half=0, own=True)
+            self.give("xb", "x", self.here, half=1, own=True)
+            self.lift(0, True)
+
+    def turn_plane(self):
+        if self.twice:
+            for other, kind in ((False, "xa"), (True, "x2")):
+                self.get(kind, "x", self.k.z, other_x=True, other_y=other)
+                self.lift(3 if other else 2)
+        else:
+            self.turn(self.here, None)
+
+    def lift_plane(self):
+        if not self.twice:
+            z = self.k.z
+            self.get("ya", "y", z, other_y=True, half=0)
+            self.lift(1)
+            self.get("xb", "x", z, other_x=True, half=1)
+            self.lift(2)
+            self.get("ya2", "y", z, other_x=True, other_y=True, half=0)
+            self.get("xb2", "x", z, other_x=True, other_y=True, half=1)
+            self.lift(3)
+
+    def along_plane(self, number, i):
+        z, exists, letter, way, goes_on = self.near()[number]
+        place = dict(other_x=i >= 2, other_y=i % 2 == 1)
+
+        @pl.when(exists())
+        def _():
+            self.get(f"{letter}{i}", way, z(), **place)
+
+        self.give(f"{letter}{i}", way, z, when=goes_on, **place)
+        self.give(f"c{i}", "core", z, when=exists, **place)
+
+    def steps(self):
+        count = 2 * (self.k.line - 1)
+        if self.z_first:
+            one = [self.start]
+            two = [lambda n=n: self.along(n) for n in range(count)]
+            spots = [(z, exists) for z, exists, _, _, _ in self.near()]
+            if not self.twice:
+                spots = [(self.here, None)] + spots
+            three = [lambda z=z, e=e: self.turn(z, e) for z, e in spots]
+            four = [lambda z=z, e=e: self.share(z, e) for z, e in spots]
+            if self.twice:
+                four = [self.share_twice] + four
+            return [one, two, three, four]
+        one = [self.start_plane]
+        two = [self.turn_plane]
+        three = [self.lift_plane]
+        four = [lambda n=n, i=i: self.along_plane(n, i) for n in range(count) for i in range(4)]
+        return [one, two, three, four]
+
+    def end(self):
+        k = self.k
+        for z in range(k.line):
+            for i in range(4):
+                k.arrive(
+                    self.spot(z, i >= 2, i % 2 == 1, core=1 - k.c), self.at(f"c{i}", z), "core"
+                )
+
+
+AG_SEMS = len(Gather.KINDS)
+
+
+def all_gather_kernel(line, swaps, cuts, piece, *refs):
+    near, out, far = refs[:swaps], refs[swaps], refs[swaps + 1 : 2 * swaps + 1]
+    send_sems, recv_sems, copy_sem = refs[2 * swaps + 1 :]
+    links = Links(line, send_sems, recv_sems)
+    links.greet(False)
+    rows = piece.shape[0] // 2
+    first_rows, second_rows = cuts
+    spare = 2 * AG_SEMS * line
+
+    def index(c, z, x, y):
+        return (((z * 2 + x) * 2 + c) * 2 + y) * rows
+
+    def keep():
+        start = index(links.c, links.z, links.x, 0)
+        return pltpu.make_async_copy(
+            piece, out.at[pl.ds(pl.multiple_of(start, 16), 2 * rows)], copy_sem
+        )
+
+    gathers = []
+
+    def own_of(first, count, cut):
+        def own(other, half):
+            begin, size = {None: (0, count), 0: (0, cut), 1: (cut, count - cut)}[half]
+            y = 1 - links.y if other else links.y
+            return piece.at[pl.ds(pl.multiple_of(y * rows + first + begin, 16), size)]
+
+        return own
+
+    last = rows - first_rows - second_rows
+    spans = ((0, first_rows + second_rows, first_rows, True), (first_rows + second_rows, last, last // 32 * 16, False))
+    for number, (first, count, cut, z_first) in enumerate(spans):
+        gathers.append(
+            Gather(
+                links, number * AG_SEMS * line, own_of(first, count, cut), out, index,
+                first, count, cut, z_first, True,
+            )
+        )
+    flat, tall = gathers[0].steps(), gathers[1].steps()
+    for step in flat[0] + tall[0]:
+        step()
+    keep().start()
+    for i in range(swaps):
+        links.send(lambda i=i: (near[i], far[i], spare + i, "y", None))
+    along, rise = flat[1], tall[1] + tall[2]
+    turn, share, climb = flat[2], flat[3], tall[3]
+    for step in along[:2] + rise + turn[:2] + along[2:4] + climb[:8] + turn[2:4] + along[4:]:
+        step()
+    for step in climb[8:16] + turn[4:] + share[:3] + climb[16:] + share[3:]:
+        step()
+    for gather in gathers:
+        gather.end()
+    keep().wait()
+    for i in range(swaps):
+        links.arrive(far[i], spare + i, "y")
+    links.finish()
+
+
+def all_gather(piece, swaps, line, collective_id):
+    any_space = pl.BlockSpec(memory_space=pl.ANY)
+    sems = 2 * AG_SEMS * line + len(swaps)
+    rows = piece.shape[0] // 2
+    cuts = (rows * 2 // 5 // 16 * 16, rows * 7 // 20 // 16 * 16)
+    return pl.pallas_call(
+        functools.partial(all_gather_kernel, line, len(swaps), cuts),
+        out_shape=[jax.ShapeDtypeStruct((4 * line * piece.shape[0], LANE), BF16)]
+        + [jax.ShapeDtypeStruct(s.shape, s.dtype) for s in swaps],
+        in_specs=[any_space] * (1 + len(swaps)),
+        out_specs=[any_space] * (1 + len(swaps)),
+        scratch_shapes=[
+            pltpu.SemaphoreType.DMA((sems,)),
+            pltpu.SemaphoreType.DMA((sems,)),
+            pltpu.SemaphoreType.DMA,
+        ],
+        compiler_params=params(32, collective_id=collective_id, has_side_effects=True),
+        cost_estimate=cost(0, 100 * MIB),
+        name="all_gather",
+    )(piece, *swaps)
+
+
+PAIRS = D // LANE
+UP_ROWS = FF * D // LANE
+REST_ROWS = 128 * LANE
+HEAD, NORM, LAST = 900, 901, 902
+ORDER = (
+    0, HEAD, 10, 100, 11, HEAD, HEAD, 12, 13, 20, 110, 111, 112, 113, HEAD, HEAD, HEAD, HEAD,
+    21, 22, 23, HEAD, HEAD, HEAD, HEAD, HEAD, NORM, LAST, 200, 210, 211, 212, 213, 30, 31, 32,
+    33, 40, 50, 60, 61, 220, 221, 222, 223, 51, 52, 70, 120, 121, 122, 123, 230, 231, 232, 233,
+    240, 250, 130, 62, 63, 131, 132, 133, 260, 261, 71, 72, 73, 251, 262, 252, 263, 140, 150,
+    160, 161, 151, 152, 162, 170, 163, 270, 271, 171, 272, 273, 172, 173, 80, 280, 180,
+)
+
+
+def segments():
+    found = [[]]
+    for step in ORDER:
+        if step >= HEAD:
+            found.append([])
+        else:
+            found[-1].append((step // 100, step // 10 % 10, step % 10))
+    return found
+
+
+def total_kinds(line):
+    kinds = []
+    for size in (UP_ROWS, UP_ROWS, REST_ROWS):
+        rows = size // (8 * line)
+        kinds.append((size, rows * 68 // 100 // 16 * 16, rows * 33 // 100 // 16 * 16))
+    return kinds
+
+
+def back_kernel(
+    line,
+    q, k, v, att, grad_att, chance, tokens, n1, att_all, resid_low, w_qkv, vec, vec_one, d_up, d_down,
+    d_first, grad_near, out, grad_back, first_back,
+    d_q, d_k, d_fresh, first_far, far, d_rest, vec_grad, flat, *scratch,
+):
+    step = pl.program_id(0)
+    buffers, (send_sems, recv_sems, load_sems, copy_sems) = scratch[:-4], scratch[-4:]
+    links = Links(line, send_sems, recv_sems)
+    tops = (REST_ROWS + UP_ROWS, REST_ROWS, 0)
+    totals = [
+        Total(
+            links, g * AR_SEMS * line, source, 0, kind, out, top,
+            buffers[7 * g : 7 * g + 7], load_sems.at[g], copy_sems.at[g],
+        )
+        for g, (source, kind, top) in enumerate(zip((d_down, d_up, d_rest), total_kinds(line), tops))
+    ]
+    spare = len(totals) * AR_SEMS * line
+    plan = segments()
+
+    def run(number):
+        for g, stage, part in plan[number]:
+            totals[g].run(stage, part)
+
+    queries = q.shape[0]
+    for head in range(2):
+        for s in range(PAIRS):
+
+            @pl.when(step == s)
+            def _(s=s, head=head):
+                if s == 0 and head == 0:
+                    links.greet(True)
+                run(2 * s + head)
+
+        @pl.when(step < PAIRS)
+        def _(head=head):
+            cols = slice(head * HD, (head + 1) * HD)
+            grad = grad_att[:, cols]
+            weights = chance[head]
+            shared = grad.astype(F32) * att[:, cols].astype(F32)
+            delta = jnp.sum(shared.T, axis=0, keepdims=True)
+            grad_chance = mm(v[:, cols], grad, NT)
+            grad_scores = (weights.astype(F32) * (grad_chance - delta)).astype(BF16)
+            grad_value = mm(weights, grad)
+
+            @pl.when(step < 3)
+            def _():
+                d_fresh[jnp.minimum(step, 2), :, cols] = grad_value.astype(BF16)
+
+            @pl.when(step >= 3)
+            def _():
+                d_first[:, cols] = grad_value[:queries]
+                first_far[jnp.maximum(step - 3, 0), :, cols] = grad_value[queries:].astype(BF16)
+
+            d_k[step, :, cols] = mm(grad_scores, q[:, cols]).astype(BF16)
+            d_q[step, :, cols] = (mm(k[:, cols], grad_scores, TN).T * HD ** (-0.5)).astype(BF16)
+
+    @pl.when(step == PAIRS)
+    def _():
+        rows = n1.shape[0] // 2
+        per_row = D // LANE
+        run(2 * PAIRS)
+        links.send(lambda: (first_far, first_back, spare, "y", None))
+        dq = jnp.concatenate([d_q[i] for i in range(PAIRS)], axis=1)
+        dk = jnp.concatenate([d_k[i] for i in range(PAIRS)], axis=1)
+        dv = jnp.concatenate([d_fresh[i] for i in range(PAIRS // 2)], axis=1)
+        grads = mm(dk, w_qkv[:, D : 2 * D], NT) + mm(dv, w_qkv[:, 2 * D :], NT)
+        beside = grads[rows:]
+        far[...] = beside.astype(BF16)
+        links.send(lambda: (far, grad_back, spare + 1, "y", None))
+        near = grads[:rows] + mm(dq, w_qkv[:, :D], NT)
+        grad_near[...] = near
+        hat, _ = normed(tokens[...].astype(F32))
+        vec_grad[...] = vec_one[...]
+        vec_grad[:, :D] = jnp.sum(near * hat[:rows], axis=0, keepdims=True) + jnp.sum(
+            beside * hat[rows:], axis=0, keepdims=True
+        )
+        vec_grad[:, D : 2 * D] = jnp.sum(near, axis=0, keepdims=True) + jnp.sum(
+            beside, axis=0, keepdims=True
+        )
+        vec_grad[:, 4 * D : 5 * D] = jnp.sum(dq.astype(F32), axis=0, keepdims=True)
+        vec_grad[:, 7 * D : 7 * D + HV] = jnp.sum(dv.astype(F32), axis=0, keepdims=True)
+        run(2 * PAIRS + 1)
+        pieces = (
+            (n1[:rows], dq, 0, per_row),
+            (n1[...], dk, D * per_row, per_row),
+            (n1[...], dv, 2 * D * per_row, HV // LANE),
+            (att_all[...], resid_low[...], 2 * D * per_row + D * HV // LANE, per_row),
+        )
+        for left, right, start, columns in pieces:
+            product = mm(left, right, TN)
+            size = D * columns
+            for j in range(columns):
+                flat[pl.ds(j, D, stride=columns), :] = product[:, j * LANE : (j + 1) * LANE]
+            d_rest[start : start + size] = flat[:size].astype(BF16)
+        flat[: 2 * LANE] = jnp.zeros((2 * LANE, LANE), F32)
+        for j in range(VEC // LANE):
+            flat[j : j + 1] = vec_grad[:, j * LANE : (j + 1) * LANE]
+        d_rest[REST:] = flat[: 2 * LANE].astype(BF16)
+        run(2 * PAIRS + 2)
+        links.arrive(first_back, spare, "y")
+        links.arrive(grad_back, spare + 1, "y")
+        links.finish()
+
+
+def back(q, k, v, att, grad_att, chance, tokens, n1, resid_low, w_qkv, vec, vec_one, d_up, d_down, line):
+    rows, keys = q.shape[0], k.shape[0]
+    any_space = pl.BlockSpec(memory_space=pl.ANY)
+
+    def column(count):
+        return pl.BlockSpec((count, LANE), lambda i: (0, jnp.minimum(i, PAIRS - 1)))
+
+    def once(array):
+        return pl.BlockSpec(array.shape, lambda i: (0,) * array.ndim, pipeline_mode=pl.Buffered(1))
+
+    kinds = total_kinds(line)
+    scratch = []
+    for size, cut, _ in kinds:
+        scratch += Scatter.buffers_of(size // (8 * line), cut, line)
+    sems = len(kinds) * AR_SEMS * line + 2
+    return pl.pallas_call(
+        functools.partial(back_kernel, line),
+        out_shape=[
+            jax.ShapeDtypeStruct((rows, HV), F32),
+            jax.ShapeDtypeStruct((rows, D), F32),
+            jax.ShapeDtypeStruct((REST_ROWS + 2 * UP_ROWS, LANE), BF16),
+            jax.ShapeDtypeStruct((rows, D), BF16),
+            jax.ShapeDtypeStruct((PAIRS // 2, rows, LANE), BF16),
+        ],
+        grid=(PAIRS + 1,),
+        in_specs=[
+            column(rows),
+            column(keys),
+            column(keys),
+            column(rows),
+            column(rows),
+            pl.BlockSpec((2, keys, rows), lambda i: (jnp.minimum(i, PAIRS - 1), 0, 0)),
+            once(tokens),
+            once(n1),
+            once(att),
+            once(resid_low),
+            once(w_qkv),
+            once(vec),
+            once(vec_one),
+            any_space,
+            any_space,
+        ],
+        out_specs=[
+            pl.BlockSpec((rows, LANE), lambda i: (0, jnp.clip(i - 3, 0, 2))),
+            pl.BlockSpec((rows, D), lambda i: (0, 0), pipeline_mode=pl.Buffered(1)),
+            any_space,
+            any_space,
+            any_space,
+        ],
+        scratch_shapes=[
+            pltpu.VMEM((PAIRS, rows, LANE), BF16),
+            pltpu.VMEM((PAIRS, keys, LANE), BF16),
+            pltpu.VMEM((PAIRS // 2, keys, LANE), BF16),
+            pltpu.VMEM((PAIRS // 2, rows, LANE), BF16),
+            pltpu.VMEM((rows, D), BF16),
+            pltpu.VMEM((REST_ROWS, LANE), BF16),
+            pltpu.VMEM((1, VEC), F32),
+            pltpu.VMEM((D * D // LANE, LANE), F32),
+        ]
+        + scratch
+        + [
+            pltpu.SemaphoreType.DMA((sems,)),
+            pltpu.SemaphoreType.DMA((sems,)),
+            pltpu.SemaphoreType.DMA((len(kinds), 4 * line)),
+            pltpu.SemaphoreType.DMA((len(kinds),)),
+        ],
+        compiler_params=params(62, collective_id=0, has_side_effects=True),
+        cost_estimate=cost(8 * rows * keys * D + 14 * rows * D * D, 100 * MIB),
+        name="back",
+    )(q, k, v, att, grad_att, chance, tokens, n1, att, resid_low, w_qkv, vec, vec_one, d_up, d_down)
+
+
 def swap(value):
     return lax.ppermute(value, "seq", [(0, 1), (1, 0)])
 
@@ -628,9 +1428,13 @@
     tokens = tokens.reshape(half_len, D)
     firsts = first_values.reshape(half_len, HV)
     given = out_grad.reshape(half_len, D)
-    tokens_far, firsts_far = swap(tokens), swap(firsts)
+    line = dp_count // 4
     packed = pack_slots(masters)
-    slots = lax.all_gather(packed, "dp", axis=0, tiled=True)
+    if line == LINE:
+        slots, tokens_far, firsts_far = all_gather(packed, [tokens, firsts], line, 1)
+    else:
+        tokens_far, firsts_far = swap(tokens), swap(firsts)
+        slots = lax.all_gather(packed, "dp", axis=0, tiled=True)
 
     slot_index = slot_numbers(owners)
     slot_rows = owners * capacity + slot_index
@@ -664,20 +1468,25 @@
     result, grad_resid, resid_low, grad_att, d_up, d_down, vec_one = hidden(
         tokens, att, given, w_out, w_up, w_down, vec
     )
-    d_q, d_k, d_fresh, d_first = attend_back(q, k, v, att, grad_att, chance)
-    grad_near, grad_far, d_rest, vec_two = project_back(
-        tokens_all, n1, d_q, d_k, d_fresh, att, resid_low, w_qkv, vec
-    )
-    grad_back = swap(grad_far)
-    first_back = swap(d_first[half_len:].astype(BF16))
-    both = ("seq", "dp")
-    grads = lax.psum(jnp.concatenate([d_rest, d_up, d_down], axis=0), both)
-    vector_total = lax.psum((vec_one + vec_two).reshape(VEC), both)
+    if line == LINE:
+        first_near, grad_near, grads, grad_back, first_back = back(
+            q, k, v, att, grad_att, chance, tokens_all, n1, resid_low, w_qkv, vec, vec_one, d_up, d_down, line
+        )
+        first_back = first_back.transpose(1, 0, 2).reshape(half_len, HV)
+    else:
+        d_q, d_k, d_fresh, d_first = attend_back(q, k, v, att, grad_att, chance)
+        grad_near, grad_far, d_rest = project_back(
+            tokens_all, n1, d_q, d_k, d_fresh, att, resid_low, w_qkv, vec, vec_one
+        )
+        first_near = d_first[:half_len]
+        grad_back, first_back = swap(grad_far), swap(d_first[half_len:].astype(BF16))
+        grads = lax.psum(jnp.concatenate([d_rest, d_up, d_down], axis=0), ("seq", "dp"))
+    vector_total = grads[REST : REST + VEC // LANE].reshape(VEC).astype(F32)
 
     grad_n1 = grad_near + grad_back.astype(F32)
     hat, rate = normed(tokens.astype(F32))
     tokens_grad = grad_resid + norm_back(grad_n1, hat, rate, vec[:, :D])
-    first_grad = d_first[:half_len] + first_back.astype(F32)
+    first_grad = first_near + first_back.astype(F32)
 
     new_master, new_one, new_two, new_low = adam(
         tile_here, grads, used, masters, moment_one, moment_two

time: 551 us -> 369 us (0.67)
  waiting for transfers between devices: 259 us -> 0 us
  Pallas kernels: 125 us -> 344 us
  blocking collectives: 78.1 us -> 0 us
  other arithmetic: 51.3 us -> 8.24 us
  between operations: 14.3 us -> 0.93 us
    pallas_call x2, Pallas kernels: 37.5 us -> 259 us  [the longest x1 160 us: back(): pl.pallas_call(functools.partial(back_kernel, line), out_shape=[jax.Shape...]
    psum x1 -> x0, waiting for transfers between devices: 154 us -> none  [shards(): grads = lax.psum(jnp.concatenate([d_rest, d_up, d_down], axis=0), both)]
    all_gather x1 -> x0, waiting for transfers between devices: 80.2 us -> none  [shards(): slots = lax.all_gather(packed, 'dp', axis=0, tiled=True)]
    psum x1 -> x0, blocking collectives: 78.1 us -> none  [shards(): vector_total = lax.psum((vec_one + vec_two).reshape(VEC), both)]
    concatenate x1 -> x0, other arithmetic: 38.2 us -> none  [shards(): grads = lax.psum(jnp.concatenate([d_rest, d_up, d_down], axis=0), both)]
    ppermute x4 -> x0, waiting for transfers between devices: 25.2 us -> none  [swap(): return lax.ppermute(value, 'seq', [(0, 1), (1, 0)])]
    unnamed x60 -> x50, local copies, waits for them, and re-layouts: 14.9 us -> 13.6 us
  transfers between devices with their start and end apart: 6 -> 0, of which waited for: 3 -> 0; matrix products, arithmetic and copies ran while one was open for 3% -> 0% of each run, Pallas kernels for 0% -> 0%
where the time goes in v4:
time: 369 us; the launch traced here: 368 us
  Pallas kernels  344 us (93%)
  local copies, waits for them, and re-layouts  15 us (4%)
  other arithmetic  8.24 us (2%)
    pallas_call x1, Pallas kernels, back(): pl.pallas_call(functools.partial(back_kernel, line), out_shape=[jax.Shape...  160 us
    pallas_call x1, Pallas kernels, all_gather(): pl.pallas_call(functools.partial(all_gather_kernel, line, len(swaps), cut...  98.3 us
    pallas_call x1, Pallas kernels, hidden(): pl.pallas_call(hidden_kernel, out_shape=[jax.ShapeDtypeStruct(line, BF16)...  31.3 us
    pallas_call x1, Pallas kernels, attend(): pl.pallas_call(attend_kernel, out_shape=[jax.ShapeDtypeStruct((queries, D...  25.2 us
    unnamed x50, local copies, waits for them, and re-layouts  13.6 us
    pallas_call x1, Pallas kernels, unpack_weights(): pl.pallas_call(unpack_kernel, out_shape=[jax.ShapeDtypeStruct(s, BF16) fo...  10.3 us
    pallas_call x1, Pallas kernels, adam(): pl.pallas_call(adam_kernel, out_shape=[jax.ShapeDtypeStruct(weight.shape,...  8.84 us
    pallas_call x1, Pallas kernels, project(): pl.pallas_call(project_kernel, out_shape=[jax.ShapeDtypeStruct((rows, D),...  7.94 us

profile of v4, /device:TPU:0, one launch (start us, length us, event | category | flops | bytes accessed | tf_op | source)
XLA Modules:
  0.0 368.0 jit_solution(5727201154861578584)
XLA Ops:
  0.7 0.8 pad_add_fusion
  1.6 0.2 copy.29
  1.9 1.7 copy-done.2
  3.6 1.7 pack_slots.1.piece
  5.3 98.3 %all_gather.1 = (bf16[81920,128]{1,0:T(8,128)(2,1)}, bf16[512,768]{1,0:T(8,128)(2,1)S(1)}, bf16[512,384]{1,0:T(8,128)(2,1)S(1)}) custom-call(bf16[5120,128]{1,0:T(8,128)(2,1)S(1)} %pack_slots.1.piece, bf16[512,768]{1,0:T(8,128)(2,1)S(1)} %bitcast.32, bf16[512,384]{1,0:T(8,128)(2,1)S(1)} %bitcast.34), custom_call_target="tpu_custom_call" | custom-call | bytes 104857600 | tf_op jit(solution)/shard_map/all_gather/pallas_call | solution.py:1179
  103.6 0.2 convert_reduce_fusion.1
  103.9 10.3 %unpack_weights.1 = (bf16[768,1920]{1,0:T(8,128)(2,1)S(1)}, bf16[768,768]{1,0:T(8,128)(2,1)S(1)}, bf16[768,3072]{1,0:T(8,128)(2,1)}, bf16[3072,768]{1,0:T(8,128)(2,1)}) custom-call(s32[414]{0:T(512)S(1)} %multiply_add_fusion.1.slot_rows, bf16[81920,128]{1,0:T(8,128)(2,1)} %get-tuple-element.41.slots), custom_call_target="tpu_custom_call" | custom-call | bytes 27131904 | tf_op jit(solution)/shard_map/unpack_weights/pallas_call | solution.py:185
  114.2 1.0 copy-done.13
  115.2 1.3 pad_maximum_fusion.tokens
  116.5 0.8 copy-done.5
  117.5 0.7 copy-done.19
  118.2 7.9 %project.1 = (bf16[1024,768]{1,0:T(8,128)(2,1)S(1)}, bf16[512,768]{1,0:T(8,128)(2,1)S(1)}, bf16[1024,768]{1,0:T(8,128)(2,1)S(1)}, bf16[1024,768]{1,0:T(8,128)(2,1)}) custom-call(bf16[1024,768]{1,0:T(8,128)(2,1)} %pad_maximum_fusion.tokens, bf16[1024,384]{1,0:T(8,128)(2,1)S(1)} %pad_maximum_fusion.1.firsts, bf16[768,1920]{1,0:T(8,128)(2,1)} %copy-done.5, ...), custom_call_target="tpu_custom_call" | custom-call | flops 3019898880 | bytes 10813440 | tf_op jit(solution)/shard_map/project/pallas_call | solution.py:226
  126.1 1.1 copy-done.7
  127.3 2.3 copy-done.9
  129.5 25.2 %attend.1 = (bf16[512,768]{1,0:T(8,128)(2,1)S(1)}, bf16[12,1024,512]{2,1,0:T(8,128)(2,1)}) custom-call(bf16[512,768]{1,0:T(8,128)(2,1)S(1)} %get-tuple-element.43.q, bf16[1024,768]{1,0:T(8,128)(2,1)S(1)} %get-tuple-element.44.k, bf16[1024,768]{1,0:T(8,128)(2,1)S(1)} %copy-done.9, s32[1,512]{1,0:T(1,128)S(1)} %bitcast.37, s32[1024,1]{1,0:T(8,128)S(1)} %bitcast.36), custom_call_target="tpu_custom_call" | custom-call | flops 1610612736 | bytes 12582912 | tf_op jit(solution)/shard_map/attend/pallas_call | solution.py:281
  154.7 0.9 copy-done.4
  155.6 31.3 %hidden.1 = (bf16[512,768]{1,0:T(8,128)(2,1)}, f32[512,768]{1,0:T(8,128)}, bf16[512,768]{1,0:T(8,128)(2,1)}, bf16[512,768]{1,0:T(8,128)(2,1)}, bf16[18432,128]{1...) custom-call(bf16[512,768]{1,0:T(8,128)(2,1)} %bitcast.31, bf16[512,768]{1,0:T(8,128)(2,1)} %copy-done.4, ...), custom_call_target="tpu_custom_call" | custom-call | flops 15703474176 | bytes 26738688 | tf_op jit(solution)/shard_map/hidden/pallas_call | solution.py:380
  186.9 160.4 %back.1 = (f32[512,384]{1,0:T(8,128)}, f32[512,768]{1,0:T(8,128)}, bf16[53248,128]{1,0:T(8,128)(2,1)}, bf16[512,768]{1,0:T(8,128)(2,1)}, bf16[3,512,128]{2,1,0:T(8,128)(2,1)}) custom-call(bf16[512,768]{1,0:T(8,128)(2,1)} %copy-done.11, bf16[1024,768]{1,0:T(8,128)(2,1)} %copy-done.8, bf16[1024,768]{1,0:T(8,128)(2,1)} %get-tuple-element.45.v, ...), custom_call_target="tpu_custom_call" | custom-call | flops 7449083904 | bytes 104857600 | tf_op jit(solution)/shard_map/back/pallas_call | solution.py:1347
  347.6 1.7 copy-done.3
  349.3 1.7 copy-done.6
  351.1 8.8 %adam.1 = (f32[40,16384]{1,0:T(8,128)}, f32[40,16384]{1,0:T(8,128)}, f32[40,16384]{1,0:T(8,128)}, bf16[40,16384]{1,0:T(8,128)(2,1)}) custom-call(s32[40]{0:T(128)S(1)} %fusion.16.places, bf16[53248,128]{1,0:T(8,128)(2,1)} %get-tuple-element.63.grads, f32[40,128]{1,0:T(8,128)S(1)} %broadcast_in_dim.26.used, f32[40,16384]{1,0:T(8,128)S(1)} %copy-done.3, ...), custom_call_target="tpu_custom_call" | custom-call | flops 13107200 | bytes 18350080 | tf_op jit(solution)/shard_map/adam/pallas_call | solution.py:580
  360.0 0.3 copy.25
  360.3 0.3 copy.26
  360.6 0.6 copy-done.17
  361.1 1.0 add_bitcast_fusion
  362.1 0.7 slice_reduce_fusion
  362.8 0.2 convert_reduce_fusion
  363.0 0.4 fusion.9
  363.4 0.7 fusion.11
  364.1 0.7 copy-done.16
  364.8 1.8 fusion.8
  366.6 1.4 multiply_subtract_fusion
  (53 shorter events, 0.8 us)
Async XLA Ops:
  1.9 1.7 copy-start.2
  3.6 1.7 copy-start
  3.6 1.7 copy-start.10
  5.3 98.3 %copy-start.22 = (s32[414]{0:T(512)S(1)}, s32[414]{0:T(512)}, u32[]{:S(2)}) copy-start(s32[414]{0:T(512)} %param.15) | copy-start | bytes 4972
  114.2 1.0 copy-start.13
  115.2 2.2 copy-start.5
  117.4 0.8 copy-start.19
  118.2 8.0 %copy-start.12 = (f32[1,8832]{1,0:T(1,128)}, f32[1,8832]{1,0:T(1,128)S(1)}, u32[]{:S(2)}) copy-start(f32[1,8832]{1,0:T(1,128)S(1)} %reshape.109.vec) | copy-start | bytes 105988
  126.1 1.1 copy-start.7
  127.3 27.5 %copy-start.8 = (bf16[1024,768]{1,0:T(8,128)(2,1)}, bf16[1024,768]{1,0:T(8,128)(2,1)S(1)}, u32[]{:S(2)}) copy-start(bf16[1024,768]{1,0:T(8,128)(2,1)S(1)} %get-tuple-element.44.k) | copy-start | bytes 4718596
  127.3 27.5 %copy-start.11 = (bf16[512,768]{1,0:T(8,128)(2,1)}, bf16[512,768]{1,0:T(8,128)(2,1)S(1)}, u32[]{:S(2)}) copy-start(bf16[512,768]{1,0:T(8,128)(2,1)S(1)} %get-tuple-element.43.q) | copy-start | bytes 2359300
  127.3 2.3 copy-start.9
  154.7 0.9 copy-start.4
  347.6 1.7 copy-start.3
  349.3 1.7 copy-start.6
  351.1 8.8 %copy-start.18 = (bf16[3,512,128]{2,1,0:T(8,128)(2,1)S(1)}, bf16[3,512,128]{2,1,0:T(8,128)(2,1)}, u32[]{:S(2)}) copy-start(bf16[3,512,128]{2,1,0:T(8,128)(2,1)} %get-tuple-element.62) | copy-start | bytes 1179652
  360.0 1.1 copy-start.17
  360.6 2.3 copy-start.1
  361.1 2.3 copy-start.14
  361.1 2.3 copy-start.15
  363.4 1.4 copy-start.16
  364.8 1.8 copy-start.20
  364.8 1.8 copy-start.21
